TPU v7x, 256 devices: a whole 4x4x8 slice. The times are simulated.
256 devices in a mesh: dp: 4 (over y_hi, core), space: 64 (over x, z, y_lo).
Axes of the slice: x: 4, y: 4 (y_hi: 2, y_lo: 2; y = y_hi * 2 + y_lo), z: 8, core: 2. Of those that a mesh axis runs over, the one named last changes fastest.
Arguments:
- fields: bfloat16 [8, 8, 128, 128, 128], P('dp', None, 'space'), may hold values from -6 to 6
- lift_weight: bfloat16 [8, 64], replicated, may hold values from -2 to 2
- mode_weight: bfloat16 [16, 256, 64, 64], P(None, 'space'), may hold values from -0.75 to 0.75
- local_weight: bfloat16 [64, 64], replicated, may hold values from -0.75 to 0.75
- project_weight: bfloat16 [64, 8], replicated, may hold values from -0.75 to 0.75
- out_cotangent: bfloat16 [8, 8, 128, 128, 128], P('dp', None, 'space'), may hold values from -6 to 6
Outputs:
- prediction: bfloat16 [8, 8, 128, 128, 128], P('dp', None, 'space')
- mode_grad: float32 [16, 256, 64, 64], P(None, 'space')
- field_grad: bfloat16 [8, 8, 128, 128, 128], P('dp', None, 'space')
All inputs are finite; a program needn't handle non-finite values.
Results may differ from a plain program's by a relative error of at most 0.025.
Values may be sent and summed in bfloat16 or wider, within the bound.
A program may use at most 128 MiB of HBM per device.

v0:
```python
import math

import jax
import jax.numpy as jnp
from jax import lax
from jax.sharding import PartitionSpec as P


def basis(count, length, start, rows, scale):
    index = start + jnp.arange(rows, dtype=jnp.int32)
    order = jnp.arange(count, dtype=jnp.int32)
    freq = (order + 1) // 2
    phase = freq[:, None] * index[None, :] % length
    angle = phase.astype(jnp.float32) * (2.0 * math.pi / length)
    wave = jnp.where((order % 2 == 0)[:, None], jnp.cos(angle), jnp.sin(angle))
    return wave * scale


def slope(value):
    normal = 0.5 * (1.0 + lax.erf(value * (1.0 / math.sqrt(2.0))))
    density = jnp.exp(-0.5 * value * value) * (1.0 / math.sqrt(2.0 * math.pi))
    return normal + value * density


def analyze(field, table_full):
    samples, width, slab, size, _ = field.shape
    modes = table_full.shape[0]
    half_full = table_full.astype(jnp.bfloat16)
    part = jnp.einsum(
        "scxyz,ky->scxkz", field, half_full, preferred_element_type=jnp.float32
    ).astype(jnp.bfloat16)
    part = jnp.einsum(
        "scxkz,jz->scxkj", part, half_full, preferred_element_type=jnp.float32
    ).astype(jnp.bfloat16)
    part = part.reshape(samples, width, slab, modes * modes)
    moved = lax.all_to_all(part, "space", split_axis=3, concat_axis=2, tiled=True)
    coef = jnp.einsum("scxm,kx->skmc", moved, half_full, preferred_element_type=jnp.float32)
    return coef.astype(jnp.bfloat16)


def synthesize(coef, table_full, table_slab):
    samples, modes, share, width = coef.shape
    slab = table_slab.shape[1]
    slab_half = table_slab.astype(jnp.bfloat16)
    planes = jnp.einsum(
        "skmd,kx->sdxm",
        lax.all_gather(coef, "space", axis=2, tiled=True),
        slab_half,
        preferred_element_type=jnp.float32,
    )
    planes = planes.reshape(samples, width, slab, modes, modes)
    inner = jnp.einsum(
        "sdxab,bz->sdxaz", planes, table_full, precision=lax.Precision.HIGHEST
    ).astype(jnp.bfloat16)
    return jnp.einsum(
        "sdxaz,ay->sdxyz",
        inner,
        table_full.astype(jnp.bfloat16),
        preferred_element_type=jnp.float32,
    )


def local(fields, lift_weight, mode_weight, local_weight, project_weight, out_cotangent):
    slab = fields.shape[2]
    size = fields.shape[3]
    modes = mode_weight.shape[0]
    first_plane = lax.axis_index("space") * slab
    ana_full = basis(modes, size, 0, size, math.sqrt(2.0 / size))
    syn_full = basis(modes, size, 0, size, math.sqrt(2.0 / modes))
    ana_slab = basis(modes, size, first_plane, slab, math.sqrt(2.0 / size))
    syn_slab = basis(modes, size, first_plane, slab, math.sqrt(2.0 / modes))
    lifted = jnp.einsum(
        "sfxyz,fc->scxyz", fields, lift_weight, preferred_element_type=jnp.float32
    ).astype(jnp.bfloat16)
    coef = analyze(lifted, ana_full)
    mixed = jnp.einsum(
        "skmc,kmcd->skmd", coef, mode_weight, preferred_element_type=jnp.float32
    ).astype(jnp.bfloat16)
    spectral = synthesize(mixed, syn_full, syn_slab)
    pre = (
        jnp.einsum("scxyz,cd->sdxyz", lifted, local_weight, preferred_element_type=jnp.float32)
        + spectral
    )
    hidden = jax.nn.gelu(pre, approximate=False).astype(jnp.bfloat16)
    prediction = jnp.einsum(
        "scxyz,cf->sfxyz", hidden, project_weight, preferred_element_type=jnp.float32
    ).astype(jnp.bfloat16)
    back_hidden = jnp.einsum(
        "sfxyz,cf->scxyz", out_cotangent, project_weight, preferred_element_type=jnp.float32
    )
    grad_pre = (back_hidden * slope(pre)).astype(jnp.bfloat16)
    coef_grad = analyze(grad_pre, syn_full)
    local_grad = jnp.einsum("skmc,skmd->kmcd", coef, coef_grad, preferred_element_type=jnp.float32)
    mode_grad = lax.psum(local_grad.astype(jnp.bfloat16), "dp").astype(jnp.float32)
    back_coef = jnp.einsum(
        "skmd,kmcd->skmc", coef_grad, mode_weight, preferred_element_type=jnp.float32
    ).astype(jnp.bfloat16)
    back_spec = synthesize(back_coef, ana_full, ana_slab)
    grad_lift = (
        jnp.einsum("sdxyz,cd->scxyz", grad_pre, local_weight, preferred_element_type=jnp.float32)
        + back_spec
    ).astype(jnp.bfloat16)
    field_grad = jnp.einsum(
        "scxyz,fc->sfxyz", grad_lift, lift_weight, preferred_element_type=jnp.float32
    ).astype(jnp.bfloat16)
    return (prediction, mode_grad, field_grad)


def solution(mesh):
    return jax.shard_map(
        local,
        mesh=mesh,
        in_specs=(
            P("dp", None, "space", None, None),
            P(),
            P(None, "space", None, None),
            P(),
            P(),
            P("dp", None, "space", None, None),
        ),
        out_specs=(
            P("dp", None, "space", None, None),
            P(None, "space", None, None),
            P("dp", None, "space", None, None),
        ),
        check_vma=False,
    )
```

profile of v0, /device:TPU:16, one launch (start us, length us, event | category | flops | bytes accessed | tf_op | source)
XLA Modules:
  0.0 872.9 jit_solution(8285393685660194898)
XLA Ops:
  7.3 1.1 copy-done
  8.4 6.3 convert_bitcast_fusion
  14.7 11.8 %convolution_convert_fusion.4 = bf16[2,64,2,16,16]{4,3,2,1,0:T(8,128)(2,1)S(1)} fusion(bf16[2,64,2,128,128]{4,1,3,2,0:T(8,128)(2,1)} %convert_bitcast_fusion, s32[16]{0:T(128)S(1)} %and_select_fusion.1, pred[16]{0:T(512)(128)(4,1)S(1)} %fusion.101), kind=kOutput, calls=%fused_computation.42 | convolution fusion | flops 151654400 | bytes 8519760 | tf_op jit(solution)/shard_map/scxkz,jz->scxkj/dot_general | solution.py:32
  26.5 12.3 %copy.38 = bf16[2,64,2,16,16]{1,4,3,2,0:T(8,128)(2,1)S(1)} copy(bf16[2,64,2,16,16]{4,3,2,1,0:T(8,128)(2,1)S(1)} %convolution_convert_fusion.4) | data formatting | bytes 262144 | tf_op jit(solution)/shard_map/convert_element_type | solution.py:34
  39.3 23.1 %all_to_all.36 = bf16[64,2,512]{2,1,0:T(2,128)(2,1)S(1)} all-to-all(bf16[64,2,512]{2,1,0:T(2,128)(2,1)S(1)} %reshape.67), channel_id=1, replica_groups=mesh['dp'=4,'space'=64] {'space'}, dimensions={0} | all-to-all | bytes 262144 | tf_op jit(solution)/shard_map/all_to_all | solution.py:36
  63.6 0.6 copy.44
  64.3 295.2 %all-gather.3.cloned.1.call-done = bf16[2,16,256,64]{3,1,0,2:T(8,128)(2,1)} async-done(((bf16[2,16,4,64]{3,1,0,2:T(8,128)(2,1)}), bf16[2,16,256,64]{3,1,0,2:T(8,128)(2,1)}) %all-gather.3.cloned.1.call-update) | async-done | bytes 1048592 | tf_op jit(solution)/shard_map/all_gather | solution.py:47
  359.5 13.6 %copy.45 = bf16[2,16,256,64]{1,2,3,0:T(8,128)(2,1)} copy(bf16[2,16,256,64]{3,1,0,2:T(8,128)(2,1)} %all-gather.3.cloned.1.call-done) | data formatting | bytes 2097152 | tf_op jit(solution)/shard_map/all_gather | solution.py:47
  373.1 5.7 convolution_bitcast_fusion.1
  379.1 1.8 copy.47
  380.9 1.9 convolution_convert_fusion.3
  382.8 8.2 fusion.86
  391.0 25.9 %bitcast_add_fusion.1 = f32[2,64,2,128,128]{4,1,3,2,0:T(8,128)} fusion(f32[128,2,64,2,128]{4,0,3,2,1:T(8,128)} %fusion.86, bf16[2,64,2,128,128]{4,1,3,2,0:T(8,128)(2,1)} %convert_bitcast_fusion, bf16[64,64]{1,0:T(8,128)(2,1)S(1)} %copy-done.2), kind=kOutput, calls=%fused_computation.13 | convolution fusion | flops 541065216 | bytes 41951232 | tf_op jit(solution)/shard_map/scxyz,cd->sdxyz/dot_general | solution.py:81
  416.9 15.2 %fusion.8 = bf16[2,64,2,128,128]{4,1,3,2,0:T(8,128)(2,1)} fusion(f32[2,64,2,128,128]{4,1,3,2,0:T(8,128)} %bitcast_add_fusion.1, bf16[2,8,2,128,128]{4,3,2,1,0:T(8,128)(2,1)S(1)} %copy-done.11, bf16[64,8]{0,1:T(8,128)(2,1)S(1)} %copy-done.14), kind=kOutput, calls=%fused_computation.10 | convolution fusion | flops 109051904 | bytes 26215424 | tf_op jit(solution)/shard_map/sfxyz,cf->scxyz/dot_general | solution.py:88
  432.1 11.8 %convolution_convert_fusion.2 = bf16[2,64,2,16,16]{4,3,2,1,0:T(8,128)(2,1)S(1)} fusion(bf16[2,64,2,128,128]{4,1,3,2,0:T(8,128)(2,1)} %fusion.8, s32[16]{0:T(128)S(1)} %and_select_fusion.1, pred[16]{0:T(512)(128)(4,1)S(1)} %fusion.101), kind=kOutput, calls=%fused_computation.40 | convolution fusion | flops 151654400 | bytes 8519760 | tf_op jit(solution)/shard_map/scxkz,jz->scxkj/dot_general | solution.py:32
  443.9 1.1 copy.51
  445.4 17.4 %all_to_all.37 = bf16[64,2,512]{2,1,0:T(2,128)(2,1)S(1)} all-to-all(bf16[64,2,512]{2,1,0:T(2,128)(2,1)S(1)} %reshape.69), channel_id=1, replica_groups=mesh['dp'=4,'space'=64] {'space'}, dimensions={0} | all-to-all | bytes 262144 | tf_op jit(solution)/shard_map/all_to_all | solution.py:36
  463.7 1.5 convolution_convert_fusion.1
  465.2 0.6 fusion.58
  465.8 0.6 copy.59
  466.5 38.0 %fusion.52 = bf16[2,8,2,128,128]{4,1,3,2,0:T(8,128)(2,1)S(1)} fusion(f32[2,64,2,128,128]{4,1,3,2,0:T(8,128)} %bitcast_add_fusion.1, bf16[64,8]{0,1:T(8,128)(2,1)S(1)} %copy-done.14), kind=kOutput, calls=%fused_computation.49 | convolution fusion | flops 340262912 | bytes 17826816 | tf_op jit(solution)/shard_map/scxyz,cf->sfxyz/dot_general | solution.py:85
  504.5 1.2 copy.64
  505.8 4.0 all-reduce.2.cloned.1.call-done
  509.7 2.8 convert_element_type.158
  512.5 300.0 %all-gather.5.cloned.1.call-done = bf16[2,16,256,64]{3,1,0,2:T(8,128)(2,1)} async-done(((bf16[2,16,4,64]{3,1,0,2:T(8,128)(2,1)}), bf16[2,16,256,64]{3,1,0,2:T(8,128)(2,1)}) %all-gather.5.cloned.1.call-update) | async-done | bytes 1048592 | tf_op jit(solution)/shard_map/all_gather | solution.py:47
  812.5 13.8 %copy.60 = bf16[2,16,256,64]{1,2,3,0:T(8,128)(2,1)} copy(bf16[2,16,256,64]{3,1,0,2:T(8,128)(2,1)} %all-gather.5.cloned.1.call-done) | data formatting | bytes 2097152 | tf_op jit(solution)/shard_map/all_gather | solution.py:47
  826.4 5.7 convolution_bitcast_fusion
  832.3 1.8 copy.62
  834.1 1.9 convolution_convert_fusion
  836.0 8.2 fusion.82
  844.3 20.6 %fusion.49 = bf16[2,8,2,128,128]{4,1,3,2,0:T(8,128)(2,1)S(1)} fusion(f32[128,2,64,2,128]{4,0,3,2,1:T(8,128)} %fusion.82, bf16[2,64,2,128,128]{4,1,3,2,0:T(8,128)(2,1)} %fusion.8, bf16[64,64]{1,0:T(8,128)(2,1)S(1)} %copy-done.3, bf16[8,64]{1,0:T(8,128)(2,1)S(1)} %copy-done.8), kind=kOutput, calls=%fused_computation.48 | convolution fusion | flops 612892672 | bytes 26223616 | tf_op jit(solution)/shard_map/scxyz,fc->sfxyz/dot_general | solution.py:103
  864.9 1.2 copy.65
  (53 shorter events, 3.6 us)
Async XLA Ops:
  7.2 1.2 copy-start
  7.2 56.0 %copy-start.12 = (bf16[16,4,64,64]{3,2,1,0:T(8,128)(2,1)S(1)}, bf16[16,4,64,64]{3,2,1,0:T(8,128)(2,1)}, u32[]{:S(2)}) copy-start(bf16[16,4,64,64]{3,2,1,0:T(8,128)(2,1)} %param.8) | copy-start | bytes 1572868
  7.2 352.3 %all-gather.3.cloned.1.call-start = ((), (), s32[]{:S(2)}) async-start(), calls=%async_computation.2 | async-start | bytes 2129920 | tf_op jit(solution)/shard_map/all_gather | solution.py:47
  7.3 456.1 %copy-start.4 = (pred[16]{0:T(512)(128)(4,1)}, pred[16]{0:T(512)(128)(4,1)S(1)}, u32[]{:S(2)}) copy-start(pred[16]{0:T(512)(128)(4,1)S(1)} %fusion.101) | copy-start | bytes 52
  8.4 455.0 %copy-start.6 = (s32[16]{0:T(128)}, s32[16]{0:T(128)S(1)}, u32[]{:S(2)}) copy-start(s32[16]{0:T(128)S(1)} %and_select_fusion.1) | copy-start | bytes 196
  64.2 445.5 %all-reduce.2.cloned.1.call-start = ((), (), s32[]{:S(2)}) async-start(), calls=%async_computation.3 | async-start | bytes 2097152 | tf_op jit(solution)/shard_map/psum | solution.py:94
  64.3 314.8 %copy-start.9 = (s32[2]{0:T(128)}, s32[2]{0:T(128)S(1)}, u32[]{:S(2)}) copy-start(s32[2]{0:T(128)S(1)} %iota_add_fusion) | copy-start | bytes 28
  373.1 17.9 %copy-start.2 = (bf16[64,64]{1,0:T(8,128)(2,1)S(1)}, bf16[64,64]{1,0:T(8,128)(2,1)}, u32[]{:S(2)}) copy-start(bf16[64,64]{1,0:T(8,128)(2,1)} %param.9) | copy-start | bytes 24580
  391.0 25.9 %copy-start.11 = (bf16[2,8,2,128,128]{4,3,2,1,0:T(8,128)(2,1)S(1)}, bf16[2,8,2,128,128]{4,3,2,1,0:T(8,128)(2,1)}, u32[]{:S(2)}) copy-start(bf16[2,8,2,128,128]{4,3,2,1,0:T(8,128)(2,1)} %param.11) | copy-start | bytes 3145732
  391.0 25.9 %copy-start.14 = (bf16[64,8]{0,1:T(8,128)(2,1)S(1)}, bf16[64,8]{0,1:T(8,128)(2,1)}, u32[]{:S(2)}) copy-start(bf16[64,8]{0,1:T(8,128)(2,1)} %param.10) | copy-start | bytes 3076
  416.9 48.3 %copy-start.13 = (bf16[16,4,64,64]{3,2,1,0:T(8,128)(2,1)S(1)}, bf16[16,4,64,64]{3,2,1,0:T(8,128)(2,1)}, u32[]{:S(2)}) copy-start(bf16[16,4,64,64]{3,2,1,0:T(8,128)(2,1)} %param.8) | copy-start | bytes 1572868
  465.1 347.4 %all-gather.5.cloned.1.call-start = ((), (), s32[]{:S(2)}) async-start(), calls=%async_computation.4 | async-start | bytes 2129920 | tf_op jit(solution)/shard_map/all_gather | solution.py:47
  466.5 359.8 %copy-start.5 = (pred[16]{0:T(512)(128)(4,1)S(1)}, pred[16]{0:T(512)(128)(4,1)}, u32[]{:S(2)}) copy-start(pred[16]{0:T(512)(128)(4,1)} %copy-done.4) | copy-start | bytes 52
  466.5 359.8 %copy-start.7 = (s32[16]{0:T(128)S(1)}, s32[16]{0:T(128)}, u32[]{:S(2)}) copy-start(s32[16]{0:T(128)} %copy-done.6) | copy-start | bytes 196
  466.5 359.8 %copy-start.10 = (s32[2]{0:T(128)S(1)}, s32[2]{0:T(128)}, u32[]{:S(2)}) copy-start(s32[2]{0:T(128)} %copy-done.9) | copy-start | bytes 28
  826.3 17.9 %copy-start.3 = (bf16[64,64]{1,0:T(8,128)(2,1)S(1)}, bf16[64,64]{1,0:T(8,128)(2,1)}, u32[]{:S(2)}) copy-start(bf16[64,64]{1,0:T(8,128)(2,1)} %param.9) | copy-start | bytes 24580
  826.4 17.9 %copy-start.8 = (bf16[8,64]{1,0:T(8,128)(2,1)S(1)}, bf16[8,64]{1,0:T(8,128)(2,1)}, u32[]{:S(2)}) copy-start(bf16[8,64]{1,0:T(8,128)(2,1)} %param.7) | copy-start | bytes 3076
  836.0 30.1 %copy-start.1 = (bf16[2,8,2,128,128]{4,3,2,1,0:T(8,128)(2,1)S(1)}, bf16[2,8,2,128,128]{4,3,2,1,0:T(8,128)(2,1)}, u32[]{:S(2)}) copy-start(bf16[2,8,2,128,128]{4,3,2,1,0:T(8,128)(2,1)} %param.6) | copy-start | bytes 3145732
Sparse Core Ops, SparseCore 0:
  64.4 295.1 all-gather.2
  465.3 44.4 all-reduce.1
  511.6 300.8 all-gather.4
where the time goes:
time: 882 us; the launch traced here: 873 us
  waiting for transfers between devices  599 us (68%)
  matrix products  164 us (19%)
  local copies, waits for them, and re-layouts  51.6 us (6%)
  blocking collectives  40.5 us (5%)
  between operations  14.3 us (2%)
    all_gather x2, waiting for transfers between devices, synthesize(): lax.all_gather(coef, 'space', axis=2, tiled=True)  595 us
    all_to_all x2, blocking collectives, analyze(): lax.all_to_all(part, 'space', split_axis=3, concat_axis=2, tiled=True)  40.5 us
    dot_general x1, matrix products, local(): jnp.einsum('scxyz,cf->sfxyz', hidden, project_weight, preferred_element_t...  38 us
    all_gather x2, local copies, waits for them, and re-layouts, synthesize(): lax.all_gather(coef, 'space', axis=2, tiled=True)  27.4 us
    dot_general x1, matrix products, local(): jnp.einsum('scxyz,cd->sdxyz', lifted, local_weight, preferred_element_typ...  25.9 us
    dot_general x2, matrix products, analyze(): jnp.einsum('scxkz,jz->scxkj', part, half_full, preferred_element_type=jnp...  23.6 us
    dot_general x1, matrix products, local(): jnp.einsum('scxyz,fc->sfxyz', grad_lift, lift_weight, preferred_element_t...  20.6 us
  transfers between devices with their start and end apart: 3, of which 3 were waited for; matrix products, arithmetic and copies ran while one was open for 5% of the time, Pallas kernels for 0%

commit v1 on v0

v1 whole, which is shorter than its diff:
```python
import math

import jax
import jax.numpy as jnp
from jax import lax
from jax.sharding import PartitionSpec as P

F32 = jnp.float32
BF = jnp.bfloat16


def basis(count, length, start, rows, scale):
    index = start + jnp.arange(rows, dtype=jnp.int32)
    order = jnp.arange(count, dtype=jnp.int32)
    freq = (order + 1) // 2
    phase = freq[:, None] * index[None, :] % length
    angle = phase.astype(jnp.float32) * (2.0 * math.pi / length)
    wave = jnp.where((order % 2 == 0)[:, None], jnp.cos(angle), jnp.sin(angle))
    return wave * scale


def slope(value):
    normal = 0.5 * (1.0 + lax.erf(value * (1.0 / math.sqrt(2.0))))
    density = jnp.exp(-0.5 * value * value) * (1.0 / math.sqrt(2.0 * math.pi))
    return normal + value * density


def ein(form, left, right):
    return jnp.einsum(form, left, right, preferred_element_type=F32)


def analyze(field, half):
    samples, width, slab, size, _ = field.shape
    modes = half.shape[0]
    part = ein("scxyz,ky->scxkz", field, half).astype(BF)
    part = ein("scxkz,jz->scxkj", part, half).astype(BF)
    part = part.reshape(samples, width, slab, modes * modes)
    moved = lax.all_to_all(part, "space", split_axis=3, concat_axis=2, tiled=True)
    return ein("scxm,kx->skmc", moved, half)


def synthesize(coef, half):
    samples, modes, share, width = coef.shape
    planes = ein("skmd,kx->sdxm", coef, half).astype(BF)
    planes = lax.all_to_all(planes, "space", split_axis=2, concat_axis=3, tiled=True)
    planes = planes.reshape(samples, width, planes.shape[2], modes, modes)
    inner = ein("sdxab,bz->sdxaz", planes, half).astype(BF)
    return ein("sdxaz,ay->sdxyz", inner, half)


def local(fields, lift_weight, mode_weight, local_weight, project_weight, out_cotangent):
    size = fields.shape[3]
    modes = mode_weight.shape[0]
    ana = basis(modes, size, 0, size, math.sqrt(2.0 / size)).astype(BF)
    syn = basis(modes, size, 0, size, math.sqrt(2.0 / modes)).astype(BF)
    both = ein("fc,cd->fd", lift_weight, local_weight).astype(BF)
    coef_field = analyze(fields, ana).astype(BF)
    coef = ein("skmf,fc->skmc", coef_field, lift_weight).astype(BF)
    mixed = ein("skmc,kmcd->skmd", coef, mode_weight).astype(BF)
    pre = ein("sfxyz,fd->sdxyz", fields, both) + synthesize(mixed, syn)
    hidden = jax.nn.gelu(pre, approximate=False).astype(BF)
    prediction = ein("scxyz,cf->sfxyz", hidden, project_weight).astype(BF)
    back_hidden = ein("sfxyz,cf->scxyz", out_cotangent, project_weight)
    grad_pre = (back_hidden * slope(pre)).astype(BF)
    coef_grad = analyze(grad_pre, syn).astype(BF)
    local_grad = ein("skmc,skmd->kmcd", coef, coef_grad)
    mode_grad = lax.psum(local_grad.astype(BF), "dp").astype(F32)
    back_coef = ein("skmd,kmcd->skmc", coef_grad, mode_weight).astype(BF)
    back_field = ein("skmc,fc->skmf", back_coef, lift_weight).astype(BF)
    field_grad = (ein("sdxyz,fd->sfxyz", grad_pre, both) + synthesize(back_field, ana)).astype(BF)
    return (prediction, mode_grad, field_grad)


def solution(mesh):
    wide = P("dp", None, "space", None, None)
    return jax.shard_map(
        local,
        mesh=mesh,
        in_specs=(wide, P(), P(None, "space", None, None), P(), P(), wide),
        out_specs=(wide, P(None, "space", None, None), wide),
        check_vma=False,
    )
```

time: 882 us -> 245 us (0.28)
  the two profiles are of different devices: /device:TPU:16 before, /device:TPU:1 now
where the time goes in v1:
time: 245 us; the launch traced here: 242 us
  matrix products  99.5 us (41%)
  waiting for transfers between devices  58.1 us (24%)
  starting transfers between devices  24.2 us (10%)
  blocking collectives  23.6 us (10%)
  local copies, waits for them, and re-layouts  18.7 us (8%)
  between operations  14.6 us (6%)
  other arithmetic  2.81 us (1%)
    dot_general x16, matrix products, ein(): return jnp.einsum(form, left, right, preferred_element_type=F32)  99.2 us
    psum x1, waiting for transfers between devices, local(): mode_grad = lax.psum(local_grad.astype(BF), 'dp').astype(F32)  41 us
    all_to_all x1, blocking collectives, analyze(): lax.all_to_all(part, 'space', split_axis=3, concat_axis=2, tiled=True)  23.6 us
    all_to_all x2, starting transfers between devices, synthesize(): lax.all_to_all(planes, 'space', split_axis=2, concat_axis=3, tiled=True)  18.5 us
    all_to_all x2, waiting for transfers between devices, synthesize(): lax.all_to_all(planes, 'space', split_axis=2, concat_axis=3, tiled=True)  17.1 us
    unnamed x34, local copies, waits for them, and re-layouts  13 us
    all_to_all x1, starting transfers between devices, analyze(): lax.all_to_all(part, 'space', split_axis=3, concat_axis=2, tiled=True)  5.67 us
  transfers between devices with their start and end apart: 4, of which 3 were waited for; matrix products, arithmetic and copies ran while one was open for 20% of the time, Pallas kernels for 0%

profile of v1, /device:TPU:1, one launch (start us, length us, event | category | flops | bytes accessed | tf_op | source)
XLA Modules:
  0.0 241.5 jit_solution(13027541632097954249)
XLA Ops:
  7.2 1.2 copy-done
  8.4 0.5 convolution_convert_fusion.5
  9.1 23.6 %all_to_all.66 = bf16[2,8,2,256]{1,2,0,3:T(2,128)(2,1)S(1)} all-to-all(bf16[2,8,2,256]{1,2,0,3:T(2,128)(2,1)S(1)} %bitcast.130), channel_id=1, replica_groups=mesh['dp'=4,'space'=64] {'space'}, dimensions={3} | all-to-all | bytes 32768 | tf_op jit(solution)/shard_map/all_to_all | solution.py:38
  33.1 1.1 convolution_convert_fusion.10
  34.2 0.6 copy-done.6
  34.8 1.6 fusion.39
  36.9 0.8 reshape.62
  37.7 7.7 %all-to-all-start.1 = ((bf16[64,2,512]{2,1,0:T(2,128)(2,1)}), bf16[64,2,512]{2,1,0:T(2,128)(2,1)S(1)}, u32[]{:S(2)}, u32[]{:S(2)}) async-start(bf16[64,2,512]{2,1,0:T(2,128)(2,1)} %reshape.62), calls=%async_computation.1 | async-start | bytes 262144 | tf_op jit(solution)/shard_map/all_to_all | solution.py:45
  45.4 0.9 fusion.43
  46.3 8.7 %all-to-all-done.1 = bf16[64,2,512]{2,1,0:T(2,128)(2,1)S(1)} async-done(((bf16[64,2,512]{2,1,0:T(2,128)(2,1)}), bf16[64,2,512]{2,1,0:T(2,128)(2,1)S(1)}, u32[]{:S(2)}, u32[]{:S(2)}) %all-to-all-start.1) | async-done | bytes 131104 | tf_op jit(solution)/shard_map/all_to_all | solution.py:45
  55.4 1.6 copy.45
  57.1 7.3 %fusion.32 = f32[128,2,64,2,128]{4,0,3,2,1:T(8,128)} fusion(bf16[2,64,2,16,16]{4,3,2,1,0:T(8,128)(2,1)S(1)} %copy.45, s32[16]{0:T(128)S(1)} %and_select_fusion, pred[16]{0:T(512)(128)(4,1)S(1)} %fusion.75), kind=kOutput, calls=%fused_computation.38 | convolution fusion | flops 151588864 | bytes 16908368 | tf_op jit(solution)/shard_map/sdxaz,ay->sdxyz/dot_general | solution.py:29
  64.4 18.1 %bitcast_add_fusion = f32[2,64,2,128,128]{4,1,3,2,0:T(8,128)S(1)} fusion(f32[128,2,64,2,128]{4,0,3,2,1:T(8,128)} %fusion.32, bf16[8,64,1,1,1]{1,0,4,3,2:T(8,128)(2,1)S(1)} %fusion.43, bf16[2,8,2,128,128]{4,3,2,1,0:T(8,128)(2,1)S(1)} %copy-done), kind=kOutput, calls=%fused_computation.11 | convolution fusion | flops 71303168 | bytes 34604032 | tf_op jit(solution)/shard_map/sfxyz,fd->sdxyz/dot_general | solution.py:29
  82.5 5.7 %copy-done.1 = f32[2,64,2,128,128]{4,1,3,2,0:T(8,128)} copy-done((f32[2,64,2,128,128]{4,1,3,2,0:T(8,128)}, f32[2,64,2,128,128]{4,1,3,2,0:T(8,128)S(1)}, u32[]{:S(2)}) %copy-start.1) | copy-done | bytes 16777240
  88.2 11.4 %fusion.8 = bf16[2,64,2,128,128]{4,1,3,2,0:T(8,128)(2,1)} fusion(f32[2,64,2,128,128]{4,1,3,2,0:T(8,128)S(1)} %bitcast_add_fusion, bf16[2,8,2,128,128]{4,3,2,1,0:T(8,128)(2,1)S(1)} %copy-done.11, bf16[64,8]{0,1:T(8,128)(2,1)S(1)} %copy-done.13), kind=kOutput, calls=%fused_computation.10 | convolution fusion | flops 109051904 | bytes 26215424 | tf_op jit(solution)/shard_map/sfxyz,cf->scxyz/dot_general | solution.py:29
  99.6 11.8 %convolution_convert_fusion.1 = bf16[2,64,2,16,16]{4,3,2,1,0:T(8,128)(2,1)S(1)} fusion(bf16[2,64,2,128,128]{4,1,3,2,0:T(8,128)(2,1)} %fusion.8, s32[16]{0:T(128)S(1)} %and_select_fusion, pred[16]{0:T(512)(128)(4,1)S(1)} %fusion.75), kind=kOutput, calls=%fused_computation.33 | convolution fusion | flops 151654400 | bytes 8519760 | tf_op jit(solution)/shard_map/scxkz,jz->scxkj/dot_general | solution.py:29
  111.4 1.1 copy.49
  112.8 0.8 reshape.64
  113.6 5.7 %all-to-all-start.2 = ((bf16[64,2,512]{2,1,0:T(2,128)(2,1)}), bf16[64,2,512]{2,1,0:T(2,128)(2,1)}, u32[]{:S(2)}, u32[]{:S(2)}) async-start(bf16[64,2,512]{2,1,0:T(2,128)(2,1)} %reshape.64), calls=%async_computation.2 | async-start | bytes 262144 | tf_op jit(solution)/shard_map/all_to_all | solution.py:38
  119.4 38.1 %fusion.33 = bf16[2,8,2,128,128]{4,1,3,2,0:T(8,128)(2,1)S(1)} fusion(f32[2,64,2,128,128]{4,1,3,2,0:T(8,128)} %copy-done.1, bf16[64,8]{0,1:T(8,128)(2,1)S(1)} %copy-done.13), kind=kOutput, calls=%fused_computation.39 | convolution fusion | flops 340262912 | bytes 17826816 | tf_op jit(solution)/shard_map/scxyz,cf->sfxyz/dot_general | solution.py:29
  157.5 1.2 copy.63
  158.7 1.1 reshape.65
  160.4 0.7 fusion.41
  161.6 0.9 copy.58
  162.4 10.8 %all-to-all-start.3 = ((bf16[2,8,128,4]{1,3,0,2:T(4,128)(2,1)}), bf16[2,8,128,4]{1,3,0,2:T(4,128)(2,1)S(1)}, u32[]{:S(2)}, u32[]{:S(2)}) async-start(bf16[2,8,128,4]{1,3,0,2:T(4,128)(2,1)} %copy.58), calls=%async_computation.3 | async-start | bytes 524288 | tf_op jit(solution)/shard_map/all_to_all | solution.py:45
  173.3 1.5 convolution_convert_fusion
  174.8 8.4 %all-to-all-done.3 = bf16[2,8,128,4]{1,3,0,2:T(4,128)(2,1)S(1)} async-done(((bf16[2,8,128,4]{1,3,0,2:T(4,128)(2,1)}), bf16[2,8,128,4]{1,3,0,2:T(4,128)(2,1)S(1)}, u32[]{:S(2)}, u32[]{:S(2)}) %all-to-all-start.3) | async-done | bytes 16416 | tf_op jit(solution)/shard_map/all_to_all | solution.py:45
  183.7 0.7 fusion.38
  184.4 5.0 %fusion.20 = bf16[2,8,2,128,128]{4,1,3,2,0:T(8,128)(2,1)S(1)} fusion(f32[128,2,8,2,128]{4,0,3,2,1:T(8,128)S(1)} %fusion.38, bf16[8,64,1,1,1]{1,0,4,3,2:T(8,128)(2,1)S(1)} %copy-done.9, bf16[2,64,2,128,128]{4,1,3,2,0:T(8,128)(2,1)} %fusion.8), kind=kOutput, calls=%fused_computation.31 | convolution fusion | flops 68157440 | bytes 11535360 | tf_op jit(solution)/shard_map/sdxyz,fd->sfxyz/dot_general | solution.py:29
  189.4 1.2 copy.64
  190.6 41.0 %all-reduce.2.cloned.1.call-done = bf16[16,4,64,64]{3,2,1,0:T(8,128)(2,1)} async-done(((bf16[16,4,64,64]{3,2,1,0:T(8,128)(2,1)}), bf16[16,4,64,64]{3,2,1,0:T(8,128)(2,1)}) %all-reduce.2.cloned.1.call-update) | async-done | bytes 524304 | tf_op jit(solution)/shard_map/psum | solution.py:67
  231.6 2.8 %convert_element_type.167 = f32[16,4,64,64]{3,2,1,0:T(8,128)} convert(bf16[16,4,64,64]{3,2,1,0:T(8,128)(2,1)} %all-reduce.2.cloned.1.call-done) | non-fusion elementwise | flops 262144 | bytes 1572864 | tf_op jit(solution)/shard_map/convert_element_type | solution.py:67
  (48 shorter events, 3.4 us)
Async XLA Ops:
  7.2 1.2 copy-start
  7.2 92.4 %copy-start.2 = (pred[16]{0:T(512)(128)(4,1)}, pred[16]{0:T(512)(128)(4,1)S(1)}, u32[]{:S(2)}) copy-start(pred[16]{0:T(512)(128)(4,1)S(1)} %fusion.75) | copy-start | bytes 52
  8.4 91.2 %copy-start.4 = (s32[16]{0:T(128)}, s32[16]{0:T(128)S(1)}, u32[]{:S(2)}) copy-start(s32[16]{0:T(128)S(1)} %and_select_fusion) | copy-start | bytes 196
  34.2 0.6 copy-start.6
  37.7 17.2 %all-to-all-start.1 = ((bf16[64,2,512]{2,1,0:T(2,128)(2,1)}), bf16[64,2,512]{2,1,0:T(2,128)(2,1)S(1)}, u32[]{:S(2)}, u32[]{:S(2)}) async-start(bf16[64,2,512]{2,1,0:T(2,128)(2,1)} %reshape.62), calls=%async_computation.1 | async-start | bytes 262144 | tf_op jit(solution)/shard_map/all_to_all | solution.py:45
  46.3 36.2 %copy-start.8 = (bf16[8,64,1,1,1]{1,0,4,3,2:T(8,128)(2,1)}, bf16[8,64,1,1,1]{1,0,4,3,2:T(8,128)(2,1)S(1)}, u32[]{:S(2)}) copy-start(bf16[8,64,1,1,1]{1,0,4,3,2:T(8,128)(2,1)S(1)} %fusion.43) | copy-start | bytes 3076
  64.4 23.8 %copy-start.11 = (bf16[2,8,2,128,128]{4,3,2,1,0:T(8,128)(2,1)S(1)}, bf16[2,8,2,128,128]{4,3,2,1,0:T(8,128)(2,1)}, u32[]{:S(2)}) copy-start(bf16[2,8,2,128,128]{4,3,2,1,0:T(8,128)(2,1)} %param.11) | copy-start | bytes 3145732
  64.4 23.8 %copy-start.13 = (bf16[64,8]{0,1:T(8,128)(2,1)S(1)}, bf16[64,8]{0,1:T(8,128)(2,1)}, u32[]{:S(2)}) copy-start(bf16[64,8]{0,1:T(8,128)(2,1)} %param.10) | copy-start | bytes 3076
  82.5 5.7 %copy-start.1 = (f32[2,64,2,128,128]{4,1,3,2,0:T(8,128)}, f32[2,64,2,128,128]{4,1,3,2,0:T(8,128)S(1)}, u32[]{:S(2)}) copy-start(f32[2,64,2,128,128]{4,1,3,2,0:T(8,128)S(1)} %bitcast_add_fusion) | copy-start | bytes 50331652
  113.6 45.1 %all-to-all-start.2 = ((bf16[64,2,512]{2,1,0:T(2,128)(2,1)}), bf16[64,2,512]{2,1,0:T(2,128)(2,1)}, u32[]{:S(2)}, u32[]{:S(2)}) async-start(bf16[64,2,512]{2,1,0:T(2,128)(2,1)} %reshape.64), calls=%async_computation.2 | async-start | bytes 262144 | tf_op jit(solution)/shard_map/all_to_all | solution.py:38
  119.3 40.8 %copy-start.3 = (pred[16]{0:T(512)(128)(4,1)S(1)}, pred[16]{0:T(512)(128)(4,1)}, u32[]{:S(2)}) copy-start(pred[16]{0:T(512)(128)(4,1)} %copy-done.2) | copy-start | bytes 52
  119.3 40.8 %copy-start.5 = (s32[16]{0:T(128)S(1)}, s32[16]{0:T(128)}, u32[]{:S(2)}) copy-start(s32[16]{0:T(128)} %copy-done.4) | copy-start | bytes 196
  119.3 41.1 %copy-start.12 = (bf16[16,4,64,64]{3,2,1,0:T(8,128)(2,1)S(1)}, bf16[16,4,64,64]{3,2,1,0:T(8,128)(2,1)}, u32[]{:S(2)}) copy-start(bf16[16,4,64,64]{3,2,1,0:T(8,128)(2,1)} %param.8) | copy-start | bytes 1572868
  119.3 41.7 %copy-start.10 = (bf16[8,64]{1,0:T(8,128)(2,1)S(1)}, bf16[8,64]{1,0:T(8,128)(2,1)}, u32[]{:S(2)}) copy-start(bf16[8,64]{1,0:T(8,128)(2,1)} %param.7) | copy-start | bytes 3076
  119.4 53.9 %copy-start.7 = (bf16[2,16,4,64]{3,1,2,0:T(8,128)(2,1)S(1)}, bf16[2,16,4,64]{3,1,2,0:T(8,128)(2,1)}, u32[]{:S(2)}) copy-start(bf16[2,16,4,64]{3,1,2,0:T(8,128)(2,1)} %copy-done.6) | copy-start | bytes 49156
  119.4 65.0 %copy-start.9 = (bf16[8,64,1,1,1]{1,0,4,3,2:T(8,128)(2,1)S(1)}, bf16[8,64,1,1,1]{1,0,4,3,2:T(8,128)(2,1)}, u32[]{:S(2)}) copy-start(bf16[8,64,1,1,1]{1,0,4,3,2:T(8,128)(2,1)} %copy-done.8) | copy-start | bytes 3076
  162.4 20.7 %all-to-all-start.3 = ((bf16[2,8,128,4]{1,3,0,2:T(4,128)(2,1)}), bf16[2,8,128,4]{1,3,0,2:T(4,128)(2,1)S(1)}, u32[]{:S(2)}, u32[]{:S(2)}) async-start(bf16[2,8,128,4]{1,3,0,2:T(4,128)(2,1)} %copy.58), calls=%async_computation.3 | async-start | bytes 524288 | tf_op jit(solution)/shard_map/all_to_all | solution.py:45
  173.2 58.4 %all-reduce.2.cloned.1.call-start = ((), (), s32[]{:S(2)}) async-start(), calls=%async_computation.4 | async-start | bytes 2097152 | tf_op jit(solution)/shard_map/psum | solution.py:67
Sparse Core Ops, SparseCore 0:
  177.3 54.2 all-reduce.1

commit v2 on v1

v2 whole, which is shorter than its diff:
```python
import functools
import math

import jax
import jax.numpy as jnp
import ml_dtypes
import numpy as np
from jax import lax
from jax.experimental import pallas as pl
from jax.experimental.pallas import tpu as pltpu
from jax.sharding import PartitionSpec as P

F32 = jnp.float32
BF = jnp.bfloat16
MESH = pl.DeviceIdType.MESH

GRID = 128
FIELDS = 8
CH = 64
MODES = 16
PIX = GRID * GRID
ROWS = 32
TILE = 512
ANA = 1.0 / 512.0
SYN = 8.0 ** -1.5


def dot(a, b, dims=((1,), (0,))):
    return lax.dot_general(a, b, (dims, ((), ())), preferred_element_type=F32)


def waves():
    order = np.arange(MODES)
    angle = 2.0 * np.pi * ((order[:, None] + 1) // 2 * np.arange(GRID)[None, :] % GRID) / GRID
    return np.where((order % 2 == 0)[:, None], np.cos(angle), np.sin(angle))


def half(x):
    return np.asarray(x, np.float32).astype(ml_dtypes.bfloat16)


def tables(space):
    w = waves()
    share = MODES * MODES // space
    row = np.arange(MODES * MODES)
    mode = share * (row % space) + row // space
    grid = (w[mode // MODES][:, :, None] * w[mode % MODES][:, None, :]).reshape(MODES * MODES, PIX)
    a0, a1 = w[:, 0::2], w[:, 1::2]
    rep0 = np.repeat(a0, 8, axis=0)
    rep1 = np.repeat(a1, 8, axis=0)
    eye = np.eye(8)
    kron = np.concatenate([np.kron(a0, eye), np.kron(a1, eye)], axis=0)
    return half(grid), half(rep0), half(rep1), half(rep0.T), half(rep1.T), half(kron), half(kron.T)


def iota(shape, axis):
    return lax.broadcasted_iota(jnp.int32, shape, axis)


def activation(v, back):
    size = jnp.abs(v)
    t = 1.0 / (1.0 + (0.3275911 / math.sqrt(2.0)) * size)
    e = jnp.exp2((v * v) * (-0.5 / math.log(2.0)))
    poly = 0.5 * 1.061405429
    for c in (-1.453152027, 1.421413741, -0.284496736, 0.254829592):
        poly = poly * t + 0.5 * c
    tail = poly * t * e
    normal = jnp.where(v >= 0.0, 1.0 - tail, tail)
    hidden = v * normal
    grad = back * (normal + v * (e * (1.0 / math.sqrt(2.0 * math.pi))))
    return hidden, grad


def exchange(src, dst, send_sem, recv_sem, me, space):
    def body(step, carry):
        to = lax.rem(me + step, space)
        pltpu.make_async_remote_copy(
            src_ref=src.at[to],
            dst_ref=dst.at[me],
            send_sem=send_sem,
            recv_sem=recv_sem,
            device_id={"space": to},
            device_id_type=MESH,
        ).start()
        return carry

    lax.fori_loop(1, space, body, 0)
    dst[me] = src[me]


def arrive(src, dst, send_sem, recv_sem, me, space):
    whole = pltpu.make_async_remote_copy(
        src_ref=src.at[pl.ds(0, space - 1)],
        dst_ref=dst.at[pl.ds(0, space - 1)],
        send_sem=send_sem,
        recv_sem=recv_sem,
        device_id={"space": lax.rem(me + 1, space)},
        device_id_type=MESH,
    )
    whole.wait_send()
    whole.wait_recv()


def kernel(
    space, dp,
    f_hbm, c_hbm, w_hbm, t_hbm, lift_ref, local_ref, project_ref,
    rep0_ref, rep1_ref, rep0t_ref, rep1t_ref, kron_ref, kront_ref,
    pred_hbm, mode_hbm, field_hbm,
    t_ref, w_ref, raw_f, raw_c, wide, flat_f, flat_c, part, out_p, out_f, mode_out,
    pre_s, back_s, hid_s, grad_s, acc, planes, rows_s, stack,
    send1, recv1, send2, recv2, send3, recv3, send4, recv4, team, team_w,
    load_sem, store_sem, send_sem, recv_sem,
):
    me = lax.axis_index("space")
    my_dp = lax.axis_index("dp")
    share = MODES * MODES // space
    chunks = 8
    width = PIX // chunks

    load_f = pltpu.make_async_copy(f_hbm, raw_f, load_sem.at[0])
    load_f.start()
    load_t = []
    for n in range(chunks):
        cut = pl.ds(n * width, width)
        load_t.append(pltpu.make_async_copy(t_hbm.at[:, cut], t_ref.at[:, cut], load_sem.at[3 + n]))
        load_t[-1].start()
    load_c = pltpu.make_async_copy(c_hbm, raw_c, load_sem.at[1])
    load_c.start()
    load_w = pltpu.make_async_copy(w_hbm, w_ref, load_sem.at[2])
    load_w.start()

    barrier = pltpu.get_barrier_semaphore()

    def greet(step, carry):
        pl.semaphore_signal(barrier, inc=1, device_id={"space": lax.rem(me + step, space)}, device_id_type=MESH)
        return carry

    lax.fori_loop(1, space, greet, 0)
    for step in range(1, dp):
        pl.semaphore_signal(barrier, inc=1, device_id={"dp": lax.rem(my_dp + step, dp)}, device_id_type=MESH)

    lift = lift_ref[...]
    pick32 = (iota((ROWS, FIELDS), 0) // 2 % FIELDS == iota((ROWS, FIELDS), 1)).astype(F32).astype(BF)
    pick128 = (iota((128, FIELDS), 0) // 2 % FIELDS == iota((128, FIELDS), 1)).astype(F32).astype(BF)
    p_row, q_lane = iota((ROWS, 256), 0), iota((ROWS, 256), 1)
    same = (p_row // 16 == q_lane // 128) & (p_row % 2 == q_lane // CH % 2)
    both = dot(lift, local_ref[...]).astype(BF)
    both32 = dot(pick32, both)
    both32 = jnp.where(same, jnp.concatenate([both32] * 4, axis=1), 0.0)
    proj32 = dot(pick32, project_ref[...])
    proj32 = jnp.where(same, jnp.concatenate([proj32] * 4, axis=1), 0.0)
    down_field = both32.astype(BF)
    down_proj = proj32.astype(BF)
    up_field = both32.T.astype(BF)
    up_proj = proj32.T.astype(BF)
    lift128 = dot(pick128, lift)
    lift_big = jnp.concatenate([lift128] * 4, axis=1)
    lift_bigt = lift_big.T.astype(BF)
    lift_big = lift_big.astype(BF)
    r128, l128 = iota((128, 128), 0), iota((128, 128), 1)
    mask_field = (r128 % 4 == l128 // 32) & (r128 // 4 % 2 == l128 // 16 % 2)
    first_plane = l128 % 2 == 0
    r256, l256 = iota((128, 256), 0), iota((128, 256), 1)
    mask_mode = r256 % 4 == l256 // CH

    def relayout(raw, flat):
        def widen(n, carry):
            cut = pl.ds(n * 4, 4)
            wide[pl.ds(pl.multiple_of(n * 512, 512), 512), :] = raw[cut].astype(F32).reshape(512, 128)
            return carry

        lax.fori_loop(0, 8, widen, 0)

        def turn(n, carry):
            for u in range(8):
                y = n * 8 + u
                rows = wide[pl.ds(y, ROWS, stride=GRID), :]
                flat[:, pl.ds(pl.multiple_of(y * GRID, GRID), GRID)] = rows.astype(BF)
            return carry

        lax.fori_loop(0, GRID // 8, turn, 0)

    load_f.wait()
    relayout(raw_f, flat_f)
    spec = None
    for n in range(chunks):
        load_t[n].wait()
        cut = pl.ds(n * width, width)
        term = dot(t_ref[:, cut], flat_f[:, cut], ((1,), (1,)))
        spec = term if spec is None else spec + term
    send1[...] = jnp.concatenate([spec[b * space:(b + 1) * space] for b in range(share)], axis=1).reshape(space, 1, 128)

    pl.semaphore_wait(barrier, space - 1 + dp - 1)
    exchange(send1, recv1, send_sem.at[0], recv_sem.at[0], me, space)
    load_c.wait()
    relayout(raw_c, flat_c)
    load_w.wait()
    arrive(send1, recv1, send_sem.at[0], recv_sem.at[0], me, space)

    got = recv1[...].reshape(space, 128).astype(BF)
    coef = jnp.where(first_plane, dot(rep0_ref[...], got), dot(rep1_ref[...], got)) * ANA
    coef = jnp.where(mask_field, coef, 0.0).astype(BF)
    coef = dot(coef, lift_big)
    team_w[:, 0:CH] = coef[:, 0:CH]
    stack[...] = jnp.where(mask_mode, coef, 0.0)
    mixed = []
    for k in range(MODES):
        mixed.append(dot(stack[k * 8:k * 8 + 8, :].astype(BF), w_ref[k]))
    mixed = (jnp.concatenate(mixed, axis=0) * SYN).astype(BF)
    out = jnp.concatenate(
        [dot(kront_ref[:, 0:128], mixed), dot(kront_ref[:, 128:256], mixed)], axis=1
    )
    send2[...] = out.reshape(space, 8, 128).astype(BF)
    exchange(send2, recv2, send_sem.at[1], recv_sem.at[1], me, space)
    acc[...] = jnp.zeros_like(acc)
    arrive(send2, recv2, send_sem.at[1], recv_sem.at[1], me, space)

    rows_s[...] = recv2[...].astype(F32).reshape(space * 8, 128)
    for s in range(2):
        for b in range(share):
            block = rows_s[pl.ds(s * 4 + b, space, stride=8), :]
            planes[s * 128:(s + 1) * 128, b * space:(b + 1) * space] = block.T.astype(BF)

    def tile(n, carry):
        cut = pl.ds(pl.multiple_of(n * TILE, TILE), TILE)
        pre_s[...] = dot(planes[...], t_ref[:, cut]) + dot(up_field, flat_f[:, cut])
        back_s[...] = dot(up_proj, flat_c[:, cut])
        for r in range(0, 256, 16):
            hidden, grad = activation(pre_s[r:r + 16, :], back_s[r:r + 16, :])
            hid_s[r:r + 16, :] = hidden.astype(BF)
            grad_s[r:r + 16, :] = grad.astype(BF)
        guess = dot(down_proj, hid_s[...])
        local = dot(down_field, grad_s[...])
        for u in range(TILE // GRID):
            y = n * (TILE // GRID) + u
            wide[pl.ds(y, ROWS, stride=GRID), :] = guess[:, u * GRID:(u + 1) * GRID]
            part[pl.ds(y, ROWS, stride=GRID), :] = local[:, u * GRID:(u + 1) * GRID]
        acc[...] += dot(t_ref[:, cut], grad_s[...], ((1,), (1,)))
        return carry

    lax.fori_loop(0, PIX // TILE, tile, 0)

    for s in range(2):
        for b in range(share):
            rows_s[pl.ds(s * 4 + b, space, stride=8), :] = acc[b * space:(b + 1) * space, s * 128:(s + 1) * 128]
    send3[...] = rows_s[...].reshape(space, 8, 128).astype(BF)
    exchange(send3, recv3, send_sem.at[2], recv_sem.at[2], me, space)

    def narrow(src, dst):
        def body(n, carry):
            dst[pl.ds(n * 4, 4)] = src[pl.ds(pl.multiple_of(n * 512, 512), 512), :].reshape(4, 128, 128).astype(BF)
            return carry

        lax.fori_loop(0, 8, body, 0)

    narrow(wide, out_p)
    store_p = pltpu.make_async_copy(out_p, pred_hbm, store_sem.at[0])
    store_p.start()
    arrive(send3, recv3, send_sem.at[2], recv_sem.at[2], me, space)

    got = recv3[...].astype(F32).reshape(space * 8, 128).astype(BF)
    full = dot(kron_ref[...], got)
    cgrad = (full[0:128, 0:CH] + full[128:256, CH:128]) * SYN
    team_w[:, CH:128] = cgrad
    back = []
    for k in range(MODES):
        back.append(dot(cgrad[k * 8:k * 8 + 8, :].astype(BF), w_ref[k], ((1,), (1,))))
    back = jnp.where(mask_mode, jnp.concatenate(back, axis=0), 0.0).astype(BF)
    back = jnp.where(mask_field, dot(back, lift_bigt) * ANA, 0.0).astype(BF)
    lanes = iota((space, 128), 1)
    out = jnp.where(lanes % 2 == 0, dot(rep0t_ref[...], back), dot(rep1t_ref[...], back))
    send4[...] = out.reshape(space, 1, 128)
    exchange(send4, recv4, send_sem.at[3], recv_sem.at[3], me, space)

    team[my_dp] = team_w[...].astype(BF)
    copies = []
    for step in range(1, dp):
        copies.append(pltpu.make_async_remote_copy(
            src_ref=team.at[my_dp],
            dst_ref=team.at[my_dp],
            send_sem=send_sem.at[3 + step],
            recv_sem=recv_sem.at[3 + step],
            device_id={"dp": lax.rem(my_dp + step, dp)},
            device_id_type=MESH,
        ))
        copies[-1].start()
    for copy in copies:
        copy.wait()
    m_row, m_lane = iota((32, 256), 0), iota((32, 256), 1)
    mask_team = m_row % 4 == m_lane // CH
    for k in range(MODES):
        rows = jnp.concatenate([team[d].astype(F32)[k * 8:k * 8 + 8, :] for d in range(dp)], axis=0)
        left = jnp.where(mask_team, jnp.concatenate([rows[:, 0:CH]] * 4, axis=1), 0.0)
        mode_out[k] = dot(left.T.astype(BF), rows[:, CH:128].astype(BF))
    store_m = pltpu.make_async_copy(mode_out, mode_hbm, store_sem.at[1])
    store_m.start()
    arrive(send4, recv4, send_sem.at[3], recv_sem.at[3], me, space)

    turned = recv4[...].reshape(space, 128).T
    field = jnp.concatenate([turned[b * 32:(b + 1) * 32] for b in range(share)], axis=1).astype(BF)

    def last(n, carry):
        cut = pl.ds(pl.multiple_of(n * TILE, TILE), TILE)
        value = dot(field, t_ref[:, cut])
        for u in range(TILE // GRID):
            at = pl.ds(n * (TILE // GRID) + u, ROWS, stride=GRID)
            part[at, :] = part[at, :] + value[:, u * GRID:(u + 1) * GRID]
        return carry

    lax.fori_loop(0, PIX // TILE, last, 0)
    narrow(part, out_f)
    store_f = pltpu.make_async_copy(out_f, field_hbm, store_sem.at[2])
    store_f.start()
    store_p.wait()
    store_m.wait()
    store_f.wait()


def solution(mesh):
    space, dp = mesh.shape["space"], mesh.shape["dp"]
    consts = tables(space)

    def local(fields, lift_weight, mode_weight, local_weight, project_weight, out_cotangent):
        planes = (ROWS, GRID, GRID)
        hbm = pl.BlockSpec(memory_space=pl.ANY)
        vmem = pl.BlockSpec(memory_space=pltpu.VMEM)
        share = MODES * MODES // space
        prediction, mode_grad, field_grad = pl.pallas_call(
            functools.partial(kernel, space, dp),
            out_shape=(
                jax.ShapeDtypeStruct(planes, BF),
                jax.ShapeDtypeStruct((MODES, share * CH, CH), F32),
                jax.ShapeDtypeStruct(planes, BF),
            ),
            in_specs=[hbm] * 4 + [vmem] * 9,
            out_specs=(hbm, hbm, hbm),
            scratch_shapes=[
                pltpu.VMEM((256, PIX), BF),
                pltpu.VMEM((MODES, share * CH, CH), BF),
                pltpu.VMEM(planes, BF),
                pltpu.VMEM(planes, BF),
                pltpu.VMEM((ROWS * GRID, GRID), F32),
                pltpu.VMEM((ROWS, PIX), BF),
                pltpu.VMEM((ROWS, PIX), BF),
                pltpu.VMEM((ROWS * GRID, GRID), F32),
                pltpu.VMEM(planes, BF),
                pltpu.VMEM(planes, BF),
                pltpu.VMEM((MODES, share * CH, CH), F32),
                pltpu.VMEM((256, TILE), F32),
                pltpu.VMEM((256, TILE), F32),
                pltpu.VMEM((256, TILE), BF),
                pltpu.VMEM((256, TILE), BF),
                pltpu.VMEM((256, 256), F32),
                pltpu.VMEM((256, 256), BF),
                pltpu.VMEM((space * 8, 128), F32),
                pltpu.VMEM((128, 256), F32),
                pltpu.VMEM((space, 1, 128), F32),
                pltpu.VMEM((space, 1, 128), F32),
                pltpu.VMEM((space, 8, 128), BF),
                pltpu.VMEM((space, 8, 128), BF),
                pltpu.VMEM((space, 8, 128), BF),
                pltpu.VMEM((space, 8, 128), BF),
                pltpu.VMEM((space, 1, 128), F32),
                pltpu.VMEM((space, 1, 128), F32),
                pltpu.VMEM((dp, 128, 128), BF),
                pltpu.VMEM((128, 128), F32),
                pltpu.SemaphoreType.DMA((11,)),
                pltpu.SemaphoreType.DMA((3,)),
                pltpu.SemaphoreType.DMA((3 + dp,)),
                pltpu.SemaphoreType.DMA((3 + dp,)),
            ],
            compiler_params=pltpu.CompilerParams(
                collective_id=0, has_side_effects=True, vmem_limit_bytes=56 * 1024 * 1024
            ),
        )(
            fields.reshape(planes),
            out_cotangent.reshape(planes),
            mode_weight.reshape(MODES, share * CH, CH),
            jnp.asarray(consts[0]),
            lift_weight,
            local_weight,
            project_weight.T,
            *[jnp.asarray(c) for c in consts[1:]],
        )
        return (
            prediction.reshape(fields.shape),
            mode_grad.reshape(mode_weight.shape),
            field_grad.reshape(fields.shape),
        )

    wide = P("dp", None, "space", None, None)
    return jax.shard_map(
        local,
        mesh=mesh,
        in_specs=(wide, P(), P(None, "space", None, None), P(), P(), wide),
        out_specs=(wide, P(None, "space", None, None), wide),
        check_vma=False,
    )
```

time: 245 us -> 89.9 us (0.37); the launches traced: 242 us -> 89.7 us
  matrix products: 99.5 us -> 0 us
  Pallas kernels: 0 us -> 83.7 us
  waiting for transfers between devices: 58.1 us -> 0 us
  starting transfers between devices: 24.2 us -> 0 us
  blocking collectives: 23.6 us -> 0 us
  between operations: 14.6 us -> 0.65 us
  local copies, waits for them, and re-layouts: 18.7 us -> 5.39 us
  other arithmetic: 2.81 us -> 0 us
    dot_general x16 -> x0, matrix products: 99.2 us -> none  [ein(): return jnp.einsum(form, left, right, preferred_element_type=F32)]
    pallas_call x0 -> x1, Pallas kernels: none -> 83.7 us  [local(): pl.pallas_call(functools.partial(kernel, space, dp), out_shape=(jax.Shape...]
    psum x1 -> x0, waiting for transfers between devices: 41 us -> none  [local(): mode_grad = lax.psum(local_grad.astype(BF), 'dp').astype(F32)]
    all_to_all x3 -> x0, starting transfers between devices: 24.1 us -> none  [the longest x2 18.5 us: synthesize(): lax.all_to_all(planes, 'space', split_axis=2, concat_axis=3, tiled=True)]
    all_to_all x1 -> x0, blocking collectives: 23.6 us -> none  [analyze(): lax.all_to_all(part, 'space', split_axis=3, concat_axis=2, tiled=True)]
    all_to_all x3 -> x0, waiting for transfers between devices: 17.1 us -> none  [the longest x2 17.1 us: synthesize(): lax.all_to_all(planes, 'space', split_axis=2, concat_axis=3, tiled=True)]
    unnamed x34 -> x7, local copies, waits for them, and re-layouts: 13 us -> 5.39 us
    convert_element_type x2 -> x0, other arithmetic: 2.8 us -> none  [the longest x1 2.79 us: local(): mode_grad = lax.psum(local_grad.astype(BF), 'dp').astype(F32)]
  transfers between devices with their start and end apart: 4 -> 0, of which waited for: 3 -> 0; matrix products, arithmetic and copies ran while one was open for 20% -> 0% of each run, Pallas kernels for 0% -> 0%
where the time goes in v2:
time: 89.9 us; the launch traced here: 89.7 us
  Pallas kernels  83.7 us (93%)
  local copies, waits for them, and re-layouts  5.39 us (6%)
    pallas_call x1, Pallas kernels, local(): pl.pallas_call(functools.partial(kernel, space, dp), out_shape=(jax.Shape...  83.7 us
    unnamed x7, local copies, waits for them, and re-layouts  5.39 us

profile of v2, /device:TPU:1, one launch (start us, length us, event | category | flops | bytes accessed | tf_op | source)
XLA Modules:
  0.0 89.7 jit_solution(7774278962782007959)
XLA Ops:
  0.6 83.7 %shard_map.148 = (bf16[32,128,128]{2,1,0:T(8,128)(2,1)}, f32[16,256,64]{2,1,0:T(8,128)}, bf16[32,128,128]{2,1,0:T(8,128)(2,1)}) custom-call(bf16[32,128,128]{2,1,0:T(8,128)(2,1)} %bitcast.10, bf16[32,128,128]{2,1,0:T(8,128)(2,1)} %bitcast.11, bf16[16,256,64]{2,1,0:T(8,128)(2,1)} %bitcast.12, bf16[256,16384]{1,0:T(8,128)(2,1)} %constant.14.clone.t_hbm, ...), custom_call_target="tpu_custom_call" | custom-call | tf_op jit(solution)/shard_map/pallas_call | solution.py:328
  84.3 0.0 copy-start
  84.3 2.5 %copy.19 = bf16[2,8,2,128,128]{4,3,2,1,0:T(8,128)(2,1)} copy(bf16[2,8,2,128,128]{4,3,2,1,0:T(8,128)(2,1)} %bitcast.9) | data formatting | bytes 2097152
  86.8 0.0 copy-done
  86.8 0.0 copy-start.1
  86.8 1.3 %copy.20 = f32[16,4,64,64]{3,2,1,0:T(8,128)} copy(f32[16,4,64,64]{3,2,1,0:T(8,128)S(1)} %bitcast.7) | data formatting | bytes 2097152
  88.1 0.6 copy-done.1
  88.7 1.0 %copy.21 = bf16[2,8,2,128,128]{4,3,2,1,0:T(8,128)(2,1)} copy(bf16[2,8,2,128,128]{4,3,2,1,0:T(8,128)(2,1)S(1)} %bitcast.8) | data formatting | bytes 2097152
Async XLA Ops:
  84.3 2.5 %copy-start = (f32[16,256,64]{2,1,0:T(8,128)S(1)}, f32[16,256,64]{2,1,0:T(8,128)}, u32[]{:S(2)}) copy-start(f32[16,256,64]{2,1,0:T(8,128)} %get-tuple-element.7) | copy-start | bytes 3145732
  86.8 2.0 %copy-start.1 = (bf16[32,128,128]{2,1,0:T(8,128)(2,1)S(1)}, bf16[32,128,128]{2,1,0:T(8,128)(2,1)}, u32[]{:S(2)}) copy-start(bf16[32,128,128]{2,1,0:T(8,128)(2,1)} %get-tuple-element.8) | copy-start | bytes 3145732

commit v3 on v2

--- a/solution.py
+++ b/solution.py
@@ -20,7 +20,7 @@
 MODES = 16
 PIX = GRID * GRID
 ROWS = 32
-TILE = 512
+TILE = 1024
 ANA = 1.0 / 512.0
 SYN = 8.0 ** -1.5
 
@@ -49,8 +49,10 @@
     rep0 = np.repeat(a0, 8, axis=0)
     rep1 = np.repeat(a1, 8, axis=0)
     eye = np.eye(8)
+    wave_z = w[mode % MODES]
+    pair_y = np.kron(np.eye(2), w)
     kron = np.concatenate([np.kron(a0, eye), np.kron(a1, eye)], axis=0)
-    return half(grid), half(rep0), half(rep1), half(rep0.T), half(rep1.T), half(kron), half(kron.T)
+    return half(grid), half(rep0), half(rep1), half(rep0.T), half(rep1.T), half(kron), half(kron.T), half(wave_z), half(pair_y), half(pair_y.T)
 
 
 def iota(shape, axis):
@@ -58,22 +60,27 @@
 
 
 def activation(v, back):
-    size = jnp.abs(v)
-    t = 1.0 / (1.0 + (0.3275911 / math.sqrt(2.0)) * size)
+    normal = 0.5 + 0.5 * lax.erf(v * math.sqrt(0.5))
     e = jnp.exp2((v * v) * (-0.5 / math.log(2.0)))
-    poly = 0.5 * 1.061405429
-    for c in (-1.453152027, 1.421413741, -0.284496736, 0.254829592):
-        poly = poly * t + 0.5 * c
-    tail = poly * t * e
-    normal = jnp.where(v >= 0.0, 1.0 - tail, tail)
-    hidden = v * normal
     grad = back * (normal + v * (e * (1.0 / math.sqrt(2.0 * math.pi))))
-    return hidden, grad
+    return v * normal, grad
+
+
+def hops(step):
+    x, z, y = step
+    return min(x, 4 - x) + min(z, 8 - z) + y
+
+
+STEPS = sorted(
+    [(x, z, y) for x in range(4) for z in range(8) for y in range(2) if x or z or y],
+    key=hops, reverse=True,
+)
 
 
 def exchange(src, dst, send_sem, recv_sem, me, space):
-    def body(step, carry):
-        to = lax.rem(me + step, space)
+    x, z, y = me // 16, me // 2 % 8, me % 2
+    for dx, dz, dy in STEPS:
+        to = lax.rem(x + dx, 4) * 16 + lax.rem(z + dz, 8) * 2 + lax.rem(y + dy, 2)
         pltpu.make_async_remote_copy(
             src_ref=src.at[to],
             dst_ref=dst.at[me],
@@ -82,9 +89,6 @@
             device_id={"space": to},
             device_id_type=MESH,
         ).start()
-        return carry
-
-    lax.fori_loop(1, space, body, 0)
     dst[me] = src[me]
 
 
@@ -104,10 +108,10 @@
 def kernel(
     space, dp,
     f_hbm, c_hbm, w_hbm, t_hbm, lift_ref, local_ref, project_ref,
-    rep0_ref, rep1_ref, rep0t_ref, rep1t_ref, kron_ref, kront_ref,
-    pred_hbm, mode_hbm, field_hbm,
-    t_ref, w_ref, raw_f, raw_c, wide, flat_f, flat_c, part, out_p, out_f, mode_out,
-    pre_s, back_s, hid_s, grad_s, acc, planes, rows_s, stack,
+    rep0_ref, rep1_ref, rep0t_ref, rep1t_ref, kron_ref, kront_ref, wavez_ref, pairy_ref,
+    pred_hbm, part_hbm, last_ref, team_ref,
+    t_ref, w_ref, raw_f, raw_c, wide, flat_f, flat_c, part, out_p, out_f, part_y,
+    pre_a, back_a, hid_a, grad_a, pre_b, back_b, hid_b, grad_b, acc, planes, rows_s, stack,
     send1, recv1, send2, recv2, send3, recv3, send4, recv4, team, team_w,
     load_sem, store_sem, send_sem, recv_sem,
 ):
@@ -181,17 +185,19 @@
         lax.fori_loop(0, GRID // 8, turn, 0)
 
     load_f.wait()
-    relayout(raw_f, flat_f)
-    spec = None
-    for n in range(chunks):
-        load_t[n].wait()
-        cut = pl.ds(n * width, width)
-        term = dot(t_ref[:, cut], flat_f[:, cut], ((1,), (1,)))
-        spec = term if spec is None else spec + term
+    for n in range(ROWS // 2):
+        pair = raw_f[2 * n:2 * n + 2].reshape(2 * GRID, GRID)
+        part_y[n * 32:n * 32 + 32, :] = dot(pairy_ref[...], pair).astype(BF)
+    value = dot(part_y[...], wavez_ref[...], ((1,), (1,)))
+    s_row, s_lane = iota((512, 256), 0), iota((512, 256), 1)
+    value = jnp.where(s_row % MODES == s_lane % space // share, value, 0.0).astype(BF)
+    fold = (iota((ROWS, 512), 0) == iota((ROWS, 512), 1) // MODES).astype(F32).astype(BF)
+    spec = dot(fold, value).T
     send1[...] = jnp.concatenate([spec[b * space:(b + 1) * space] for b in range(share)], axis=1).reshape(space, 1, 128)
 
     pl.semaphore_wait(barrier, space - 1 + dp - 1)
     exchange(send1, recv1, send_sem.at[0], recv_sem.at[0], me, space)
+    relayout(raw_f, flat_f)
     load_c.wait()
     relayout(raw_c, flat_c)
     load_w.wait()
@@ -213,6 +219,8 @@
     send2[...] = out.reshape(space, 8, 128).astype(BF)
     exchange(send2, recv2, send_sem.at[1], recv_sem.at[1], me, space)
     acc[...] = jnp.zeros_like(acc)
+    for copy in load_t:
+        copy.wait()
     arrive(send2, recv2, send_sem.at[1], recv_sem.at[1], me, space)
 
     rows_s[...] = recv2[...].astype(F32).reshape(space * 8, 128)
@@ -221,14 +229,21 @@
             block = rows_s[pl.ds(s * 4 + b, space, stride=8), :]
             planes[s * 128:(s + 1) * 128, b * space:(b + 1) * space] = block.T.astype(BF)
 
-    def tile(n, carry):
+    def front(n, pre_s, back_s):
         cut = pl.ds(pl.multiple_of(n * TILE, TILE), TILE)
         pre_s[...] = dot(planes[...], t_ref[:, cut]) + dot(up_field, flat_f[:, cut])
         back_s[...] = dot(up_proj, flat_c[:, cut])
+
+    def middle(pre_s, back_s, hid_s, grad_s):
         for r in range(0, 256, 16):
-            hidden, grad = activation(pre_s[r:r + 16, :], back_s[r:r + 16, :])
-            hid_s[r:r + 16, :] = hidden.astype(BF)
-            grad_s[r:r + 16, :] = grad.astype(BF)
+            for c in range(0, TILE, 256):
+                at = (slice(r, r + 16), slice(c, c + 256))
+                hidden, grad = activation(pre_s[at], back_s[at])
+                hid_s[at] = hidden.astype(BF)
+                grad_s[at] = grad.astype(BF)
+
+    def back(n, hid_s, grad_s):
+        cut = pl.ds(pl.multiple_of(n * TILE, TILE), TILE)
         guess = dot(down_proj, hid_s[...])
         local = dot(down_field, grad_s[...])
         for u in range(TILE // GRID):
@@ -236,9 +251,20 @@
             wide[pl.ds(y, ROWS, stride=GRID), :] = guess[:, u * GRID:(u + 1) * GRID]
             part[pl.ds(y, ROWS, stride=GRID), :] = local[:, u * GRID:(u + 1) * GRID]
         acc[...] += dot(t_ref[:, cut], grad_s[...], ((1,), (1,)))
+
+    tiles = PIX // TILE
+    front(0, pre_a, back_a)
+
+    def two(n, carry):
+        front(2 * n + 1, pre_b, back_b)
+        middle(pre_a, back_a, hid_a, grad_a)
+        back(2 * n, hid_a, grad_a)
+        front(jnp.minimum(2 * n + 2, tiles - 1), pre_a, back_a)
+        middle(pre_b, back_b, hid_b, grad_b)
+        back(2 * n + 1, hid_b, grad_b)
         return carry
 
-    lax.fori_loop(0, PIX // TILE, tile, 0)
+    lax.fori_loop(0, tiles // 2, two, 0)
 
     for s in range(2):
         for b in range(share):
@@ -256,6 +282,9 @@
     narrow(wide, out_p)
     store_p = pltpu.make_async_copy(out_p, pred_hbm, store_sem.at[0])
     store_p.start()
+    narrow(part, out_f)
+    store_f = pltpu.make_async_copy(out_f, part_hbm, store_sem.at[1])
+    store_f.start()
     arrive(send3, recv3, send_sem.at[2], recv_sem.at[2], me, space)
 
     got = recv3[...].astype(F32).reshape(space * 8, 128).astype(BF)
@@ -286,34 +315,54 @@
         copies[-1].start()
     for copy in copies:
         copy.wait()
+    team_ref[...] = team[...]
+    arrive(send4, recv4, send_sem.at[3], recv_sem.at[3], me, space)
+    last_ref[...] = recv4[...].reshape(space, 128)
+    store_p.wait()
+    store_f.wait()
+
+
+def finish(
+    space, dp, pred_in, part_in, last_ref, team_ref, wavez_ref, pairyt_ref,
+    pred_hbm, mode_hbm, field_hbm,
+    part, out, mode_out, inner, load_sem, store_sem,
+):
+    share = MODES * MODES // space
+    groups = 4
+    each = ROWS // groups
+    store_p = pltpu.make_async_copy(pred_in, pred_hbm, store_sem.at[0])
+    store_p.start()
+    load_p = pltpu.make_async_copy(part_in, part, load_sem)
+    load_p.start()
+
     m_row, m_lane = iota((32, 256), 0), iota((32, 256), 1)
     mask_team = m_row % 4 == m_lane // CH
     for k in range(MODES):
-        rows = jnp.concatenate([team[d].astype(F32)[k * 8:k * 8 + 8, :] for d in range(dp)], axis=0)
+        rows = jnp.concatenate([team_ref[d].astype(F32)[k * 8:k * 8 + 8, :] for d in range(dp)], axis=0)
         left = jnp.where(mask_team, jnp.concatenate([rows[:, 0:CH]] * 4, axis=1), 0.0)
         mode_out[k] = dot(left.T.astype(BF), rows[:, CH:128].astype(BF))
     store_m = pltpu.make_async_copy(mode_out, mode_hbm, store_sem.at[1])
     store_m.start()
-    arrive(send4, recv4, send_sem.at[3], recv_sem.at[3], me, space)
-
-    turned = recv4[...].reshape(space, 128).T
+
+    turned = last_ref[...].T
     field = jnp.concatenate([turned[b * 32:(b + 1) * 32] for b in range(share)], axis=1).astype(BF)
-
-    def last(n, carry):
-        cut = pl.ds(pl.multiple_of(n * TILE, TILE), TILE)
-        value = dot(field, t_ref[:, cut])
-        for u in range(TILE // GRID):
-            at = pl.ds(n * (TILE // GRID) + u, ROWS, stride=GRID)
-            part[at, :] = part[at, :] + value[:, u * GRID:(u + 1) * GRID]
-        return carry
-
-    lax.fori_loop(0, PIX // TILE, last, 0)
-    narrow(part, out_f)
-    store_f = pltpu.make_async_copy(out_f, field_hbm, store_sem.at[2])
-    store_f.start()
+    spread = (iota((512, ROWS), 0) // MODES == iota((512, ROWS), 1)).astype(F32).astype(BF)
+    s_row, s_lane = iota((512, 256), 0), iota((512, 256), 1)
+    value = jnp.where(s_row % MODES == s_lane % space // share, dot(spread, field), 0.0).astype(BF)
+    inner[...] = dot(value, wavez_ref[...]).astype(BF)
+    load_p.wait()
+    stores = []
+    for g in range(groups):
+        for n in range(g * each // 2, (g + 1) * each // 2):
+            value = dot(pairyt_ref[...], inner[n * 32:n * 32 + 32, :]).reshape(2, GRID, GRID)
+            out[2 * n:2 * n + 2] = (part[2 * n:2 * n + 2].astype(F32) + value).astype(BF)
+        cut = pl.ds(g * each, each)
+        stores.append(pltpu.make_async_copy(out.at[cut], field_hbm.at[cut], store_sem.at[2 + g]))
+        stores[-1].start()
     store_p.wait()
     store_m.wait()
-    store_f.wait()
+    for copy in stores:
+        copy.wait()
 
 
 def solution(mesh):
@@ -325,15 +374,17 @@
         hbm = pl.BlockSpec(memory_space=pl.ANY)
         vmem = pl.BlockSpec(memory_space=pltpu.VMEM)
         share = MODES * MODES // space
-        prediction, mode_grad, field_grad = pl.pallas_call(
+        small = [jnp.asarray(c) for c in consts[1:]]
+        guess, part, last, team = pl.pallas_call(
             functools.partial(kernel, space, dp),
             out_shape=(
                 jax.ShapeDtypeStruct(planes, BF),
-                jax.ShapeDtypeStruct((MODES, share * CH, CH), F32),
                 jax.ShapeDtypeStruct(planes, BF),
+                jax.ShapeDtypeStruct((space, 128), F32),
+                jax.ShapeDtypeStruct((dp, 128, 128), BF),
             ),
-            in_specs=[hbm] * 4 + [vmem] * 9,
-            out_specs=(hbm, hbm, hbm),
+            in_specs=[hbm] * 4 + [vmem] * 11,
+            out_specs=(hbm, hbm, vmem, vmem),
             scratch_shapes=[
                 pltpu.VMEM((256, PIX), BF),
                 pltpu.VMEM((MODES, share * CH, CH), BF),
@@ -345,7 +396,11 @@
                 pltpu.VMEM((ROWS * GRID, GRID), F32),
                 pltpu.VMEM(planes, BF),
                 pltpu.VMEM(planes, BF),
-                pltpu.VMEM((MODES, share * CH, CH), F32),
+                pltpu.VMEM((512, 128), BF),
+                pltpu.VMEM((256, TILE), F32),
+                pltpu.VMEM((256, TILE), F32),
+                pltpu.VMEM((256, TILE), BF),
+                pltpu.VMEM((256, TILE), BF),
                 pltpu.VMEM((256, TILE), F32),
                 pltpu.VMEM((256, TILE), F32),
                 pltpu.VMEM((256, TILE), BF),
@@ -365,7 +420,7 @@
                 pltpu.VMEM((dp, 128, 128), BF),
                 pltpu.VMEM((128, 128), F32),
                 pltpu.SemaphoreType.DMA((11,)),
-                pltpu.SemaphoreType.DMA((3,)),
+                pltpu.SemaphoreType.DMA((2,)),
                 pltpu.SemaphoreType.DMA((3 + dp,)),
                 pltpu.SemaphoreType.DMA((3 + dp,)),
             ],
@@ -380,8 +435,27 @@
             lift_weight,
             local_weight,
             project_weight.T,
-            *[jnp.asarray(c) for c in consts[1:]],
+            *small[:8],
         )
+        prediction, mode_grad, field_grad = pl.pallas_call(
+            functools.partial(finish, space, dp),
+            out_shape=(
+                jax.ShapeDtypeStruct(planes, BF),
+                jax.ShapeDtypeStruct((MODES, share * CH, CH), F32),
+                jax.ShapeDtypeStruct(planes, BF),
+            ),
+            in_specs=[hbm] * 2 + [vmem] * 4,
+            out_specs=(hbm, hbm, hbm),
+            scratch_shapes=[
+                pltpu.VMEM(planes, BF),
+                pltpu.VMEM(planes, BF),
+                pltpu.VMEM((MODES, share * CH, CH), F32),
+                pltpu.VMEM((512, 128), BF),
+                pltpu.SemaphoreType.DMA,
+                pltpu.SemaphoreType.DMA((6,)),
+            ],
+            compiler_params=pltpu.CompilerParams(vmem_limit_bytes=60 * 1024 * 1024),
+        )(guess, part, last, team, small[6], small[8])
         return (
             prediction.reshape(fields.shape),
             mode_grad.reshape(mode_weight.shape),

time: 89.9 us -> 91.2 us (1.014)
  Pallas kernels: 83.7 us -> 90.2 us
  local copies, waits for them, and re-layouts: 5.39 us -> 0 us
    pallas_call x0 -> x1, Pallas kernels: none -> 33.9 us  [local(): pl.pallas_call(functools.partial(finish, space, dp), out_shape=(jax.Shape...]
    pallas_call x1, Pallas kernels: 83.7 us -> 56.3 us  [local(): pl.pallas_call(functools.partial(kernel, space, dp), out_shape=(jax.Shape...]
    unnamed x7 -> x0, local copies, waits for them, and re-layouts: 5.39 us -> none
where the time goes in v3:
time: 91.2 us; the launch traced here: 90.8 us
  Pallas kernels  90.2 us (99%)
    pallas_call x1, Pallas kernels, local(): pl.pallas_call(functools.partial(kernel, space, dp), out_shape=(jax.Shape...  56.3 us
    pallas_call x1, Pallas kernels, local(): pl.pallas_call(functools.partial(finish, space, dp), out_shape=(jax.Shape...  33.9 us

profile of v3, /device:TPU:1, one launch (start us, length us, event | category | flops | bytes accessed | tf_op | source)
XLA Modules:
  0.0 90.8 jit_solution(2857104248260209926)
XLA Ops:
  0.6 56.3 %shard_map.175 = (bf16[32,128,128]{2,1,0:T(8,128)(2,1)}, bf16[32,128,128]{2,1,0:T(8,128)(2,1)}, f32[64,128]{1,0:T(8,128)}, bf16[4,128,128]{2,1,0:T(8,128)(2,1)}) custom-call(bf16[32,128,128]{2,1,0:T(8,128)(2,1)} %bitcast.7, bf16[32,128,128]{2,1,0:T(8,128)(2,1)} %bitcast.8, bf16[16,256,64]{2,1,0:T(8,128)(2,1)} %bitcast.9, ...), custom_call_target="tpu_custom_call" | custom-call | tf_op jit(solution)/shard_map/pallas_call | solution.py:378
  57.0 33.9 %shard_map.176 = (bf16[32,128,128]{2,1,0:T(8,128)(2,1)}, f32[16,256,64]{2,1,0:T(8,128)}, bf16[32,128,128]{2,1,0:T(8,128)(2,1)}) custom-call(bf16[32,128,128]{2,1,0:T(8,128)(2,1)} %get-tuple-element.10.pred_in, bf16[32,128,128]{2,1,0:T(8,128)(2,1)} %get-tuple-element.11.part_in, f32[64,128]{1,0:T(8,128)} %get-tuple-element.12.last_ref, ...), custom_call_target="tpu_custom_call" | custom-call | tf_op jit(solution)/shard_map/pallas_call | solution.py:440

commit v4 on v3

--- a/solution.py
+++ b/solution.py
@@ -111,7 +111,7 @@
     rep0_ref, rep1_ref, rep0t_ref, rep1t_ref, kron_ref, kront_ref, wavez_ref, pairy_ref,
     pred_hbm, part_hbm, last_ref, team_ref,
     t_ref, w_ref, raw_f, raw_c, wide, flat_f, flat_c, part, out_p, out_f, part_y,
-    pre_a, back_a, hid_a, grad_a, pre_b, back_b, hid_b, grad_b, acc, planes, rows_s, stack,
+    pre_a, grad_a, pre_b, grad_b, hid, bg, acc, planes, rows_s, stack,
     send1, recv1, send2, recv2, send3, recv3, send4, recv4, team, team_w,
     load_sem, store_sem, send_sem, recv_sem,
 ):
@@ -219,6 +219,14 @@
     send2[...] = out.reshape(space, 8, 128).astype(BF)
     exchange(send2, recv2, send_sem.at[1], recv_sem.at[1], me, space)
     acc[...] = jnp.zeros_like(acc)
+    tiles = PIX // TILE
+
+    def up(n, carry):
+        cut = pl.ds(pl.multiple_of(n * TILE, TILE), TILE)
+        bg[n] = dot(up_proj, flat_c[:, cut]).astype(BF)
+        return carry
+
+    lax.fori_loop(0, tiles, up, 0)
     for copy in load_t:
         copy.wait()
     arrive(send2, recv2, send_sem.at[1], recv_sem.at[1], me, space)
@@ -229,39 +237,34 @@
             block = rows_s[pl.ds(s * 4 + b, space, stride=8), :]
             planes[s * 128:(s + 1) * 128, b * space:(b + 1) * space] = block.T.astype(BF)
 
-    def front(n, pre_s, back_s):
-        cut = pl.ds(pl.multiple_of(n * TILE, TILE), TILE)
-        pre_s[...] = dot(planes[...], t_ref[:, cut]) + dot(up_field, flat_f[:, cut])
-        back_s[...] = dot(up_proj, flat_c[:, cut])
-
-    def middle(pre_s, back_s, hid_s, grad_s):
-        for r in range(0, 256, 16):
-            for c in range(0, TILE, 256):
-                at = (slice(r, r + 16), slice(c, c + 256))
-                hidden, grad = activation(pre_s[at], back_s[at])
-                hid_s[at] = hidden.astype(BF)
-                grad_s[at] = grad.astype(BF)
-
-    def back(n, hid_s, grad_s):
-        cut = pl.ds(pl.multiple_of(n * TILE, TILE), TILE)
-        guess = dot(down_proj, hid_s[...])
-        local = dot(down_field, grad_s[...])
-        for u in range(TILE // GRID):
-            y = n * (TILE // GRID) + u
-            wide[pl.ds(y, ROWS, stride=GRID), :] = guess[:, u * GRID:(u + 1) * GRID]
-            part[pl.ds(y, ROWS, stride=GRID), :] = local[:, u * GRID:(u + 1) * GRID]
-        acc[...] += dot(t_ref[:, cut], grad_s[...], ((1,), (1,)))
-
-    tiles = PIX // TILE
-    front(0, pre_a, back_a)
+    def columns(n):
+        return pl.ds(pl.multiple_of(n * TILE, TILE), TILE)
+
+    def front(n, pre_s):
+        pre_s[...] = dot(planes[...], t_ref[:, columns(n)]) + dot(up_field, flat_f[:, columns(n)])
+
+    def middle(n, pre_s, grad_s):
+        for r in range(0, 256, 32):
+            for c in range(0, TILE, 512):
+                at = (slice(r, r + 32), slice(c, c + 512))
+                hidden, grad = activation(pre_s[at], bg[(n,) + at].astype(F32))
+                hid[(n,) + at] = hidden.astype(BF)
+                grad = grad.astype(BF)
+                bg[(n,) + at] = grad
+                grad_s[at] = grad
+
+    def back(n, grad_s):
+        acc[...] += dot(t_ref[:, columns(n)], grad_s[...], ((1,), (1,)))
+
+    front(0, pre_a)
 
     def two(n, carry):
-        front(2 * n + 1, pre_b, back_b)
-        middle(pre_a, back_a, hid_a, grad_a)
-        back(2 * n, hid_a, grad_a)
-        front(jnp.minimum(2 * n + 2, tiles - 1), pre_a, back_a)
-        middle(pre_b, back_b, hid_b, grad_b)
-        back(2 * n + 1, hid_b, grad_b)
+        front(2 * n + 1, pre_b)
+        middle(2 * n, pre_a, grad_a)
+        back(2 * n, grad_a)
+        front(jnp.minimum(2 * n + 2, tiles - 1), pre_a)
+        middle(2 * n + 1, pre_b, grad_b)
+        back(2 * n + 1, grad_b)
         return carry
 
     lax.fori_loop(0, tiles // 2, two, 0)
@@ -279,6 +282,16 @@
 
         lax.fori_loop(0, 8, body, 0)
 
+    def down(n, carry):
+        guess = dot(down_proj, hid[n])
+        local = dot(down_field, bg[n])
+        for u in range(TILE // GRID):
+            y = n * (TILE // GRID) + u
+            wide[pl.ds(y, ROWS, stride=GRID), :] = guess[:, u * GRID:(u + 1) * GRID]
+            part[pl.ds(y, ROWS, stride=GRID), :] = local[:, u * GRID:(u + 1) * GRID]
+        return carry
+
+    lax.fori_loop(0, tiles, down, 0)
     narrow(wide, out_p)
     store_p = pltpu.make_async_copy(out_p, pred_hbm, store_sem.at[0])
     store_p.start()
@@ -325,16 +338,19 @@
 def finish(
     space, dp, pred_in, part_in, last_ref, team_ref, wavez_ref, pairyt_ref,
     pred_hbm, mode_hbm, field_hbm,
-    part, out, mode_out, inner, load_sem, store_sem,
+    pred, part, out, mode_out, inner, load_sem, store_sem,
 ):
     share = MODES * MODES // space
     groups = 4
     each = ROWS // groups
-    store_p = pltpu.make_async_copy(pred_in, pred_hbm, store_sem.at[0])
+    load_q = pltpu.make_async_copy(pred_in, pred, load_sem.at[1])
+    load_q.start()
+    load_p = pltpu.make_async_copy(part_in, part, load_sem.at[0])
+    load_p.start()
+
+    load_q.wait()
+    store_p = pltpu.make_async_copy(pred, pred_hbm, store_sem.at[0])
     store_p.start()
-    load_p = pltpu.make_async_copy(part_in, part, load_sem)
-    load_p.start()
-
     m_row, m_lane = iota((32, 256), 0), iota((32, 256), 1)
     mask_team = m_row % 4 == m_lane // CH
     for k in range(MODES):
@@ -398,13 +414,11 @@
                 pltpu.VMEM(planes, BF),
                 pltpu.VMEM((512, 128), BF),
                 pltpu.VMEM((256, TILE), F32),
+                pltpu.VMEM((256, TILE), BF),
                 pltpu.VMEM((256, TILE), F32),
                 pltpu.VMEM((256, TILE), BF),
-                pltpu.VMEM((256, TILE), BF),
-                pltpu.VMEM((256, TILE), F32),
-                pltpu.VMEM((256, TILE), F32),
-                pltpu.VMEM((256, TILE), BF),
-                pltpu.VMEM((256, TILE), BF),
+                pltpu.VMEM((PIX // TILE, 256, TILE), BF),
+                pltpu.VMEM((PIX // TILE, 256, TILE), BF),
                 pltpu.VMEM((256, 256), F32),
                 pltpu.VMEM((256, 256), BF),
                 pltpu.VMEM((space * 8, 128), F32),
@@ -449,9 +463,10 @@
             scratch_shapes=[
                 pltpu.VMEM(planes, BF),
                 pltpu.VMEM(planes, BF),
+                pltpu.VMEM(planes, BF),
                 pltpu.VMEM((MODES, share * CH, CH), F32),
                 pltpu.VMEM((512, 128), BF),
-                pltpu.SemaphoreType.DMA,
+                pltpu.SemaphoreType.DMA((2,)),
                 pltpu.SemaphoreType.DMA((6,)),
             ],
             compiler_params=pltpu.CompilerParams(vmem_limit_bytes=60 * 1024 * 1024),

time: 91.2 us -> 58.1 us (0.64)
  Pallas kernels: 90.2 us -> 57.3 us
    pallas_call x1, Pallas kernels: 33.9 us -> 4.72 us  [local(): pl.pallas_call(functools.partial(finish, space, dp), out_shape=(jax.Shape...]
    pallas_call x1, Pallas kernels: 56.3 us -> 52.6 us  [local(): pl.pallas_call(functools.partial(kernel, space, dp), out_shape=(jax.Shape...]
where the time goes in v4:
time: 58.1 us; the launch traced here: 58 us
  Pallas kernels  57.3 us (99%)
  between operations  0.64 us (1%)
    pallas_call x1, Pallas kernels, local(): pl.pallas_call(functools.partial(kernel, space, dp), out_shape=(jax.Shape...  52.6 us
    pallas_call x1, Pallas kernels, local(): pl.pallas_call(functools.partial(finish, space, dp), out_shape=(jax.Shape...  4.72 us

profile of v4, /device:TPU:1, one launch (start us, length us, event | category | flops | bytes accessed | tf_op | source)
XLA Modules:
  0.0 58.0 jit_solution(16348506122757746235)
XLA Ops:
  0.6 52.6 %shard_map.175 = (bf16[32,128,128]{2,1,0:T(8,128)(2,1)}, bf16[32,128,128]{2,1,0:T(8,128)(2,1)}, f32[64,128]{1,0:T(8,128)}, bf16[4,128,128]{2,1,0:T(8,128)(2,1)}) custom-call(bf16[32,128,128]{2,1,0:T(8,128)(2,1)} %bitcast.7, bf16[32,128,128]{2,1,0:T(8,128)(2,1)} %bitcast.8, bf16[16,256,64]{2,1,0:T(8,128)(2,1)} %bitcast.9, ...), custom_call_target="tpu_custom_call" | custom-call | tf_op jit(solution)/shard_map/pallas_call | solution.py:394
  53.2 4.7 %shard_map.176 = (bf16[32,128,128]{2,1,0:T(8,128)(2,1)}, f32[16,256,64]{2,1,0:T(8,128)}, bf16[32,128,128]{2,1,0:T(8,128)(2,1)}) custom-call(bf16[32,128,128]{2,1,0:T(8,128)(2,1)} %get-tuple-element.10.pred_in, bf16[32,128,128]{2,1,0:T(8,128)(2,1)} %get-tuple-element.11.part_in, f32[64,128]{1,0:T(8,128)} %get-tuple-element.12.last_ref, ...), custom_call_target="tpu_custom_call" | custom-call | tf_op jit(solution)/shard_map/pallas_call | solution.py:454

commit v5 on v4

--- a/solution.py
+++ b/solution.py
@@ -23,6 +23,7 @@
 TILE = 1024
 ANA = 1.0 / 512.0
 SYN = 8.0 ** -1.5
+ROOT = math.sqrt(0.5)
 
 
 def dot(a, b, dims=((1,), (0,))):
@@ -59,11 +60,11 @@
     return lax.broadcasted_iota(jnp.int32, shape, axis)
 
 
-def activation(v, back):
-    normal = 0.5 + 0.5 * lax.erf(v * math.sqrt(0.5))
-    e = jnp.exp2((v * v) * (-0.5 / math.log(2.0)))
-    grad = back * (normal + v * (e * (1.0 / math.sqrt(2.0 * math.pi))))
-    return v * normal, grad
+def activation(w, back):
+    twice = 1.0 + lax.erf(w)
+    e = jnp.exp2((w * w) * (-1.0 / math.log(2.0)))
+    slope = twice + w * (e * (2.0 / math.sqrt(math.pi)))
+    return (w * twice).astype(BF), slope.astype(BF) * back
 
 
 def hops(step):
@@ -77,10 +78,13 @@
 )
 
 
+def peers(me):
+    x, z, y = me // 16, me // 2 % 8, me % 2
+    return [lax.rem(x + dx, 4) * 16 + lax.rem(z + dz, 8) * 2 + lax.rem(y + dy, 2) for dx, dz, dy in STEPS]
+
+
 def exchange(src, dst, send_sem, recv_sem, me, space):
-    x, z, y = me // 16, me // 2 % 8, me % 2
-    for dx, dz, dy in STEPS:
-        to = lax.rem(x + dx, 4) * 16 + lax.rem(z + dz, 8) * 2 + lax.rem(y + dy, 2)
+    for to in peers(me):
         pltpu.make_async_remote_copy(
             src_ref=src.at[to],
             dst_ref=dst.at[me],
@@ -107,13 +111,14 @@
 
 def kernel(
     space, dp,
-    f_hbm, c_hbm, w_hbm, t_hbm, lift_ref, local_ref, project_ref,
-    rep0_ref, rep1_ref, rep0t_ref, rep1t_ref, kron_ref, kront_ref, wavez_ref, pairy_ref,
-    pred_hbm, part_hbm, last_ref, team_ref,
-    t_ref, w_ref, raw_f, raw_c, wide, flat_f, flat_c, part, out_p, out_f, part_y,
+    f_hbm, c_hbm, w_hbm, t_hbm, lift_hbm, local_hbm, project_hbm,
+    rep0_hbm, rep1_hbm, rep0t_hbm, rep1t_hbm, kron_hbm, kront_hbm, wavez_hbm, pairy_hbm,
+    pred_ref, part_ref, last_ref, team_ref,
+    t_ref, w_ref, raw_f, raw_c, wide, flat_f, flat_c, part, part_y,
     pre_a, grad_a, pre_b, grad_b, hid, bg, acc, planes, rows_s, stack,
     send1, recv1, send2, recv2, send3, recv3, send4, recv4, team, team_w,
-    load_sem, store_sem, send_sem, recv_sem,
+    lift_ref, local_ref, project_ref, rep0_ref, rep1_ref, rep0t_ref, rep1t_ref, kron_ref, kront_ref, wavez_ref, pairy_ref,
+    load_sem, send_sem, recv_sem,
 ):
     me = lax.axis_index("space")
     my_dp = lax.axis_index("dp")
@@ -123,6 +128,18 @@
 
     load_f = pltpu.make_async_copy(f_hbm, raw_f, load_sem.at[0])
     load_f.start()
+    load_z = pltpu.make_async_copy(wavez_hbm, wavez_ref, load_sem.at[3 + chunks])
+    load_z.start()
+    load_y = pltpu.make_async_copy(pairy_hbm, pairy_ref, load_sem.at[4 + chunks])
+    load_y.start()
+    load_s = []
+    for n, (src, dst) in enumerate([
+        (lift_hbm, lift_ref), (local_hbm, local_ref), (project_hbm, project_ref),
+        (rep0_hbm, rep0_ref), (rep1_hbm, rep1_ref), (rep0t_hbm, rep0t_ref), (rep1t_hbm, rep1t_ref),
+        (kron_hbm, kron_ref), (kront_hbm, kront_ref),
+    ]):
+        load_s.append(pltpu.make_async_copy(src, dst, load_sem.at[5 + chunks + n]))
+        load_s[-1].start()
     load_t = []
     for n in range(chunks):
         cut = pl.ds(n * width, width)
@@ -135,28 +152,59 @@
 
     barrier = pltpu.get_barrier_semaphore()
 
-    def greet(step, carry):
-        pl.semaphore_signal(barrier, inc=1, device_id={"space": lax.rem(me + step, space)}, device_id_type=MESH)
-        return carry
-
-    lax.fori_loop(1, space, greet, 0)
+    for to in peers(me):
+        pl.semaphore_signal(barrier, inc=1, device_id={"space": to}, device_id_type=MESH)
     for step in range(1, dp):
         pl.semaphore_signal(barrier, inc=1, device_id={"dp": lax.rem(my_dp + step, dp)}, device_id_type=MESH)
 
+    def relayout(raw, flat):
+        def widen(n, carry):
+            cut = pl.ds(n * 4, 4)
+            wide[pl.ds(pl.multiple_of(n * 512, 512), 512), :] = raw[cut].astype(F32).reshape(512, 128)
+            return carry
+
+        lax.fori_loop(0, 8, widen, 0)
+
+        def turn(n, carry):
+            for u in range(8):
+                y = n * 8 + u
+                rows = wide[pl.ds(y, ROWS, stride=GRID), :]
+                flat[:, pl.ds(pl.multiple_of(y * GRID, GRID), GRID)] = rows.astype(BF)
+            return carry
+
+        lax.fori_loop(0, GRID // 8, turn, 0)
+
+    load_f.wait()
+    load_z.wait()
+    load_y.wait()
+    for n in range(ROWS // 2):
+        pair = raw_f[2 * n:2 * n + 2].reshape(2 * GRID, GRID)
+        part_y[n * 32:n * 32 + 32, :] = dot(pairy_ref[...], pair).astype(BF)
+    value = dot(part_y[...], wavez_ref[...], ((1,), (1,)))
+    s_row, s_lane = iota((512, 256), 0), iota((512, 256), 1)
+    value = jnp.where(s_row % MODES == s_lane % space // share, value, 0.0).astype(BF)
+    fold = (iota((ROWS, 512), 0) == iota((ROWS, 512), 1) // MODES).astype(F32).astype(BF)
+    spec = dot(fold, value).T
+    send1[...] = jnp.concatenate([spec[b * space:(b + 1) * space] for b in range(share)], axis=1).reshape(space, 1, 128)
+
+    pl.semaphore_wait(barrier, space - 1 + dp - 1)
+    exchange(send1, recv1, send_sem.at[0], recv_sem.at[0], me, space)
+    for copy in load_s:
+        copy.wait()
     lift = lift_ref[...]
     pick32 = (iota((ROWS, FIELDS), 0) // 2 % FIELDS == iota((ROWS, FIELDS), 1)).astype(F32).astype(BF)
     pick128 = (iota((128, FIELDS), 0) // 2 % FIELDS == iota((128, FIELDS), 1)).astype(F32).astype(BF)
     p_row, q_lane = iota((ROWS, 256), 0), iota((ROWS, 256), 1)
     same = (p_row // 16 == q_lane // 128) & (p_row % 2 == q_lane // CH % 2)
-    both = dot(lift, local_ref[...]).astype(BF)
-    both32 = dot(pick32, both)
-    both32 = jnp.where(same, jnp.concatenate([both32] * 4, axis=1), 0.0)
+    both = dot(lift, local_ref[...])
+    both = jnp.concatenate([both[n // 2 % FIELDS:n // 2 % FIELDS + 1] for n in range(ROWS)], axis=0)
+    both32 = jnp.where(same, jnp.concatenate([both] * 4, axis=1), 0.0)
     proj32 = dot(pick32, project_ref[...])
     proj32 = jnp.where(same, jnp.concatenate([proj32] * 4, axis=1), 0.0)
     down_field = both32.astype(BF)
     down_proj = proj32.astype(BF)
-    up_field = both32.T.astype(BF)
-    up_proj = proj32.T.astype(BF)
+    up_field = (both32 * ROOT).T.astype(BF)
+    up_proj = (proj32 * 0.5).T.astype(BF)
     lift128 = dot(pick128, lift)
     lift_big = jnp.concatenate([lift128] * 4, axis=1)
     lift_bigt = lift_big.T.astype(BF)
@@ -167,36 +215,6 @@
     r256, l256 = iota((128, 256), 0), iota((128, 256), 1)
     mask_mode = r256 % 4 == l256 // CH
 
-    def relayout(raw, flat):
-        def widen(n, carry):
-            cut = pl.ds(n * 4, 4)
-            wide[pl.ds(pl.multiple_of(n * 512, 512), 512), :] = raw[cut].astype(F32).reshape(512, 128)
-            return carry
-
-        lax.fori_loop(0, 8, widen, 0)
-
-        def turn(n, carry):
-            for u in range(8):
-                y = n * 8 + u
-                rows = wide[pl.ds(y, ROWS, stride=GRID), :]
-                flat[:, pl.ds(pl.multiple_of(y * GRID, GRID), GRID)] = rows.astype(BF)
-            return carry
-
-        lax.fori_loop(0, GRID // 8, turn, 0)
-
-    load_f.wait()
-    for n in range(ROWS // 2):
-        pair = raw_f[2 * n:2 * n + 2].reshape(2 * GRID, GRID)
-        part_y[n * 32:n * 32 + 32, :] = dot(pairy_ref[...], pair).astype(BF)
-    value = dot(part_y[...], wavez_ref[...], ((1,), (1,)))
-    s_row, s_lane = iota((512, 256), 0), iota((512, 256), 1)
-    value = jnp.where(s_row % MODES == s_lane % space // share, value, 0.0).astype(BF)
-    fold = (iota((ROWS, 512), 0) == iota((ROWS, 512), 1) // MODES).astype(F32).astype(BF)
-    spec = dot(fold, value).T
-    send1[...] = jnp.concatenate([spec[b * space:(b + 1) * space] for b in range(share)], axis=1).reshape(space, 1, 128)
-
-    pl.semaphore_wait(barrier, space - 1 + dp - 1)
-    exchange(send1, recv1, send_sem.at[0], recv_sem.at[0], me, space)
     relayout(raw_f, flat_f)
     load_c.wait()
     relayout(raw_c, flat_c)
@@ -212,7 +230,7 @@
     mixed = []
     for k in range(MODES):
         mixed.append(dot(stack[k * 8:k * 8 + 8, :].astype(BF), w_ref[k]))
-    mixed = (jnp.concatenate(mixed, axis=0) * SYN).astype(BF)
+    mixed = (jnp.concatenate(mixed, axis=0) * (SYN * ROOT)).astype(BF)
     out = jnp.concatenate(
         [dot(kront_ref[:, 0:128], mixed), dot(kront_ref[:, 128:256], mixed)], axis=1
     )
@@ -247,9 +265,8 @@
         for r in range(0, 256, 32):
             for c in range(0, TILE, 512):
                 at = (slice(r, r + 32), slice(c, c + 512))
-                hidden, grad = activation(pre_s[at], bg[(n,) + at].astype(F32))
-                hid[(n,) + at] = hidden.astype(BF)
-                grad = grad.astype(BF)
+                hidden, grad = activation(pre_s[at], bg[(n,) + at])
+                hid[(n,) + at] = hidden
                 bg[(n,) + at] = grad
                 grad_s[at] = grad
 
@@ -283,7 +300,7 @@
         lax.fori_loop(0, 8, body, 0)
 
     def down(n, carry):
-        guess = dot(down_proj, hid[n])
+        guess = dot(down_proj, hid[n]) * ROOT
         local = dot(down_field, bg[n])
         for u in range(TILE // GRID):
             y = n * (TILE // GRID) + u
@@ -292,12 +309,6 @@
         return carry
 
     lax.fori_loop(0, tiles, down, 0)
-    narrow(wide, out_p)
-    store_p = pltpu.make_async_copy(out_p, pred_hbm, store_sem.at[0])
-    store_p.start()
-    narrow(part, out_f)
-    store_f = pltpu.make_async_copy(out_f, part_hbm, store_sem.at[1])
-    store_f.start()
     arrive(send3, recv3, send_sem.at[2], recv_sem.at[2], me, space)
 
     got = recv3[...].astype(F32).reshape(space * 8, 128).astype(BF)
@@ -326,31 +337,26 @@
             device_id_type=MESH,
         ))
         copies[-1].start()
+    narrow(wide, pred_ref)
+    narrow(part, part_ref)
     for copy in copies:
         copy.wait()
     team_ref[...] = team[...]
     arrive(send4, recv4, send_sem.at[3], recv_sem.at[3], me, space)
     last_ref[...] = recv4[...].reshape(space, 128)
-    store_p.wait()
-    store_f.wait()
 
 
 def finish(
-    space, dp, pred_in, part_in, last_ref, team_ref, wavez_ref, pairyt_ref,
+    space, dp, pred, part, last_ref, team_ref, wavez_ref, pairyt_ref,
     pred_hbm, mode_hbm, field_hbm,
-    pred, part, out, mode_out, inner, load_sem, store_sem,
+    out, mode_out, inner, store_sem,
 ):
     share = MODES * MODES // space
     groups = 4
     each = ROWS // groups
-    load_q = pltpu.make_async_copy(pred_in, pred, load_sem.at[1])
-    load_q.start()
-    load_p = pltpu.make_async_copy(part_in, part, load_sem.at[0])
-    load_p.start()
-
-    load_q.wait()
     store_p = pltpu.make_async_copy(pred, pred_hbm, store_sem.at[0])
     store_p.start()
+
     m_row, m_lane = iota((32, 256), 0), iota((32, 256), 1)
     mask_team = m_row % 4 == m_lane // CH
     for k in range(MODES):
@@ -366,7 +372,6 @@
     s_row, s_lane = iota((512, 256), 0), iota((512, 256), 1)
     value = jnp.where(s_row % MODES == s_lane % space // share, dot(spread, field), 0.0).astype(BF)
     inner[...] = dot(value, wavez_ref[...]).astype(BF)
-    load_p.wait()
     stores = []
     for g in range(groups):
         for n in range(g * each // 2, (g + 1) * each // 2):
@@ -387,20 +392,20 @@
 
     def local(fields, lift_weight, mode_weight, local_weight, project_weight, out_cotangent):
         planes = (ROWS, GRID, GRID)
-        hbm = pl.BlockSpec(memory_space=pl.ANY)
+        hbm = pl.BlockSpec(memory_space=pltpu.HBM)
         vmem = pl.BlockSpec(memory_space=pltpu.VMEM)
         share = MODES * MODES // space
         small = [jnp.asarray(c) for c in consts[1:]]
         guess, part, last, team = pl.pallas_call(
             functools.partial(kernel, space, dp),
             out_shape=(
-                jax.ShapeDtypeStruct(planes, BF),
-                jax.ShapeDtypeStruct(planes, BF),
-                jax.ShapeDtypeStruct((space, 128), F32),
-                jax.ShapeDtypeStruct((dp, 128, 128), BF),
+                pltpu.VMEM(planes, BF),
+                pltpu.VMEM(planes, BF),
+                pltpu.VMEM((space, 128), F32),
+                pltpu.VMEM((dp, 128, 128), BF),
             ),
-            in_specs=[hbm] * 4 + [vmem] * 11,
-            out_specs=(hbm, hbm, vmem, vmem),
+            in_specs=[hbm] * 15,
+            out_specs=(vmem, vmem, vmem, vmem),
             scratch_shapes=[
                 pltpu.VMEM((256, PIX), BF),
                 pltpu.VMEM((MODES, share * CH, CH), BF),
@@ -410,8 +415,6 @@
                 pltpu.VMEM((ROWS, PIX), BF),
                 pltpu.VMEM((ROWS, PIX), BF),
                 pltpu.VMEM((ROWS * GRID, GRID), F32),
-                pltpu.VMEM(planes, BF),
-                pltpu.VMEM(planes, BF),
                 pltpu.VMEM((512, 128), BF),
                 pltpu.VMEM((256, TILE), F32),
                 pltpu.VMEM((256, TILE), BF),
@@ -433,13 +436,23 @@
                 pltpu.VMEM((space, 1, 128), F32),
                 pltpu.VMEM((dp, 128, 128), BF),
                 pltpu.VMEM((128, 128), F32),
-                pltpu.SemaphoreType.DMA((11,)),
-                pltpu.SemaphoreType.DMA((2,)),
+                pltpu.VMEM((FIELDS, CH), BF),
+                pltpu.VMEM((CH, CH), BF),
+                pltpu.VMEM((FIELDS, CH), BF),
+                pltpu.VMEM((128, 64), BF),
+                pltpu.VMEM((128, 64), BF),
+                pltpu.VMEM((64, 128), BF),
+                pltpu.VMEM((64, 128), BF),
+                pltpu.VMEM((256, 512), BF),
+                pltpu.VMEM((512, 256), BF),
+                pltpu.VMEM((256, 128), BF),
+                pltpu.VMEM((32, 256), BF),
+                pltpu.SemaphoreType.DMA((22,)),
                 pltpu.SemaphoreType.DMA((3 + dp,)),
                 pltpu.SemaphoreType.DMA((3 + dp,)),
             ],
             compiler_params=pltpu.CompilerParams(
-                collective_id=0, has_side_effects=True, vmem_limit_bytes=56 * 1024 * 1024
+                collective_id=0, has_side_effects=True, vmem_limit_bytes=60 * 1024 * 1024
             ),
         )(
             fields.reshape(planes),
@@ -458,18 +471,15 @@
                 jax.ShapeDtypeStruct((MODES, share * CH, CH), F32),
                 jax.ShapeDtypeStruct(planes, BF),
             ),
-            in_specs=[hbm] * 2 + [vmem] * 4,
+            in_specs=[vmem] * 6,
             out_specs=(hbm, hbm, hbm),
             scratch_shapes=[
                 pltpu.VMEM(planes, BF),
-                pltpu.VMEM(planes, BF),
-                pltpu.VMEM(planes, BF),
                 pltpu.VMEM((MODES, share * CH, CH), F32),
                 pltpu.VMEM((512, 128), BF),
-                pltpu.SemaphoreType.DMA((2,)),
                 pltpu.SemaphoreType.DMA((6,)),
             ],
-            compiler_params=pltpu.CompilerParams(vmem_limit_bytes=60 * 1024 * 1024),
+            compiler_params=pltpu.CompilerParams(vmem_limit_bytes=32 * 1024 * 1024),
         )(guess, part, last, team, small[6], small[8])
         return (
             prediction.reshape(fields.shape),

time: 58.1 us -> 52.5 us (0.904)
  Pallas kernels: 57.3 us -> 51.7 us
    pallas_call x1, Pallas kernels: 52.6 us -> 49 us  [local(): pl.pallas_call(functools.partial(kernel, space, dp), out_shape=(pltpu.VME...]
    pallas_call x1, Pallas kernels: 4.72 us -> 2.71 us  [local(): pl.pallas_call(functools.partial(finish, space, dp), out_shape=(jax.Shape...]
where the time goes in v5:
time: 52.5 us; the launch traced here: 52.4 us
  Pallas kernels  51.7 us (98%)
  between operations  0.67 us (1%)
    pallas_call x1, Pallas kernels, local(): pl.pallas_call(functools.partial(kernel, space, dp), out_shape=(pltpu.VME...  49 us
    pallas_call x1, Pallas kernels, local(): pl.pallas_call(functools.partial(finish, space, dp), out_shape=(jax.Shape...  2.71 us

profile of v5, /device:TPU:1, one launch (start us, length us, event | category | flops | bytes accessed | tf_op | source)
XLA Modules:
  0.0 52.4 jit_solution(14726771460028501471)
XLA Ops:
  0.6 0.0 copy-start
  0.6 0.0 copy-start.1
  0.7 49.0 %shard_map.175 = (bf16[32,128,128]{2,1,0:T(8,128)(2,1)S(1)}, bf16[32,128,128]{2,1,0:T(8,128)(2,1)S(1)}, f32[64,128]{1,0:T(8,128)S(1)}, bf16[4,128,128]{2,1,0:T(8,128)(2,1)S(1)}) custom-call(bf16[32,128,128]{2,1,0:T(8,128)(2,1)} %bitcast.7, bf16[32,128,128]{2,1,0:T(8,128)(2,1)} %bitcast.8, bf16[16,256,64]{2,1,0:T(8,128)(2,1)} %bitcast.9, ...), custom_call_target="tpu_custom_call" | custom-call | tf_op jit(solution)/shard_map/pallas_call | solution.py:399
  49.7 0.0 copy-done
  49.7 0.0 copy-done.1
  49.7 2.7 %shard_map.176 = (bf16[32,128,128]{2,1,0:T(8,128)(2,1)}, f32[16,256,64]{2,1,0:T(8,128)}, bf16[32,128,128]{2,1,0:T(8,128)(2,1)}) custom-call(bf16[32,128,128]{2,1,0:T(8,128)(2,1)S(1)} %get-tuple-element.10.pred, bf16[32,128,128]{2,1,0:T(8,128)(2,1)S(1)} %get-tuple-element.11.part, f32[64,128]{1,0:T(8,128)S(1)} %get-tuple-element.12.last_ref, ...), custom_call_target="tpu_custom_call" | custom-call | tf_op jit(solution)/shard_map/pallas_call | solution.py:467
Async XLA Ops:
  0.6 49.1 %copy-start = (bf16[256,128]{1,0:T(8,128)(2,1)S(1)}, bf16[256,128]{1,0:T(8,128)(2,1)}, u32[]{:S(2)}) copy-start(bf16[256,128]{1,0:T(8,128)(2,1)} %constant.26.clone.wavez_hbm.wavez_ref) | copy-start | bytes 196612
  0.6 49.1 %copy-start.1 = (bf16[256,32]{1,0:T(8,128)(2,1)S(1)}, bf16[256,32]{1,0:T(8,128)(2,1)}, u32[]{:S(2)}) copy-start(bf16[256,32]{1,0:T(8,128)(2,1)} %constant.28.clone.pairyt_ref) | copy-start | bytes 49156

commit v6 on v5

--- a/solution.py
+++ b/solution.py
@@ -113,7 +113,7 @@
     space, dp,
     f_hbm, c_hbm, w_hbm, t_hbm, lift_hbm, local_hbm, project_hbm,
     rep0_hbm, rep1_hbm, rep0t_hbm, rep1t_hbm, kron_hbm, kront_hbm, wavez_hbm, pairy_hbm,
-    pred_ref, part_ref, last_ref, team_ref,
+    pred_ref, part_ref, last_ref, mode_ref,
     t_ref, w_ref, raw_f, raw_c, wide, flat_f, flat_c, part, part_y,
     pre_a, grad_a, pre_b, grad_b, hid, bg, acc, planes, rows_s, stack,
     send1, recv1, send2, recv2, send3, recv3, send4, recv4, team, team_w,
@@ -299,32 +299,24 @@
 
         lax.fori_loop(0, 8, body, 0)
 
-    def down(n, carry):
-        guess = dot(down_proj, hid[n]) * ROOT
-        local = dot(down_field, bg[n])
+    def down(n, maps, values, target, scale):
+        value = dot(maps, values[n]) * scale
         for u in range(TILE // GRID):
             y = n * (TILE // GRID) + u
-            wide[pl.ds(y, ROWS, stride=GRID), :] = guess[:, u * GRID:(u + 1) * GRID]
-            part[pl.ds(y, ROWS, stride=GRID), :] = local[:, u * GRID:(u + 1) * GRID]
+            target[pl.ds(y, ROWS, stride=GRID), :] = value[:, u * GRID:(u + 1) * GRID]
+
+    def down_p(n, carry):
+        down(n, down_proj, hid, wide, ROOT)
         return carry
 
-    lax.fori_loop(0, tiles, down, 0)
+    lax.fori_loop(0, tiles, down_p, 0)
+    narrow(wide, pred_ref)
     arrive(send3, recv3, send_sem.at[2], recv_sem.at[2], me, space)
 
     got = recv3[...].astype(F32).reshape(space * 8, 128).astype(BF)
     full = dot(kron_ref[...], got)
     cgrad = (full[0:128, 0:CH] + full[128:256, CH:128]) * SYN
     team_w[:, CH:128] = cgrad
-    back = []
-    for k in range(MODES):
-        back.append(dot(cgrad[k * 8:k * 8 + 8, :].astype(BF), w_ref[k], ((1,), (1,))))
-    back = jnp.where(mask_mode, jnp.concatenate(back, axis=0), 0.0).astype(BF)
-    back = jnp.where(mask_field, dot(back, lift_bigt) * ANA, 0.0).astype(BF)
-    lanes = iota((space, 128), 1)
-    out = jnp.where(lanes % 2 == 0, dot(rep0t_ref[...], back), dot(rep1t_ref[...], back))
-    send4[...] = out.reshape(space, 1, 128)
-    exchange(send4, recv4, send_sem.at[3], recv_sem.at[3], me, space)
-
     team[my_dp] = team_w[...].astype(BF)
     copies = []
     for step in range(1, dp):
@@ -337,19 +329,38 @@
             device_id_type=MESH,
         ))
         copies[-1].start()
-    narrow(wide, pred_ref)
+    back = []
+    for k in range(MODES):
+        back.append(dot(cgrad[k * 8:k * 8 + 8, :].astype(BF), w_ref[k], ((1,), (1,))))
+    back = jnp.where(mask_mode, jnp.concatenate(back, axis=0), 0.0).astype(BF)
+    back = jnp.where(mask_field, dot(back, lift_bigt) * ANA, 0.0).astype(BF)
+    lanes = iota((space, 128), 1)
+    out = jnp.where(lanes % 2 == 0, dot(rep0t_ref[...], back), dot(rep1t_ref[...], back))
+    send4[...] = out.reshape(space, 1, 128)
+    exchange(send4, recv4, send_sem.at[3], recv_sem.at[3], me, space)
+
+    def down_f(n, carry):
+        down(n, down_field, bg, part, 1.0)
+        return carry
+
+    lax.fori_loop(0, tiles, down_f, 0)
     narrow(part, part_ref)
     for copy in copies:
         copy.wait()
-    team_ref[...] = team[...]
+    m_row, m_lane = iota((32, 256), 0), iota((32, 256), 1)
+    mask_team = m_row % 4 == m_lane // CH
+    for k in range(MODES):
+        rows = jnp.concatenate([team[d].astype(F32)[k * 8:k * 8 + 8, :] for d in range(dp)], axis=0)
+        left = jnp.where(mask_team, jnp.concatenate([rows[:, 0:CH]] * 4, axis=1), 0.0)
+        mode_ref[k] = dot(left.T.astype(BF), rows[:, CH:128].astype(BF))
     arrive(send4, recv4, send_sem.at[3], recv_sem.at[3], me, space)
     last_ref[...] = recv4[...].reshape(space, 128)
 
 
 def finish(
-    space, dp, pred, part, last_ref, team_ref, wavez_ref, pairyt_ref,
+    space, pred, part, last_ref, mode_in, wavez_ref, pairyt_ref,
     pred_hbm, mode_hbm, field_hbm,
-    out, mode_out, inner, store_sem,
+    out, inner, store_sem,
 ):
     share = MODES * MODES // space
     groups = 4
@@ -357,13 +368,7 @@
     store_p = pltpu.make_async_copy(pred, pred_hbm, store_sem.at[0])
     store_p.start()
 
-    m_row, m_lane = iota((32, 256), 0), iota((32, 256), 1)
-    mask_team = m_row % 4 == m_lane // CH
-    for k in range(MODES):
-        rows = jnp.concatenate([team_ref[d].astype(F32)[k * 8:k * 8 + 8, :] for d in range(dp)], axis=0)
-        left = jnp.where(mask_team, jnp.concatenate([rows[:, 0:CH]] * 4, axis=1), 0.0)
-        mode_out[k] = dot(left.T.astype(BF), rows[:, CH:128].astype(BF))
-    store_m = pltpu.make_async_copy(mode_out, mode_hbm, store_sem.at[1])
+    store_m = pltpu.make_async_copy(mode_in, mode_hbm, store_sem.at[1])
     store_m.start()
 
     turned = last_ref[...].T
@@ -396,13 +401,13 @@
         vmem = pl.BlockSpec(memory_space=pltpu.VMEM)
         share = MODES * MODES // space
         small = [jnp.asarray(c) for c in consts[1:]]
-        guess, part, last, team = pl.pallas_call(
+        guess, part, last, mode = pl.pallas_call(
             functools.partial(kernel, space, dp),
             out_shape=(
                 pltpu.VMEM(planes, BF),
                 pltpu.VMEM(planes, BF),
                 pltpu.VMEM((space, 128), F32),
-                pltpu.VMEM((dp, 128, 128), BF),
+                pltpu.VMEM((MODES, share * CH, CH), F32),
             ),
             in_specs=[hbm] * 15,
             out_specs=(vmem, vmem, vmem, vmem),
@@ -452,7 +457,7 @@
                 pltpu.SemaphoreType.DMA((3 + dp,)),
             ],
             compiler_params=pltpu.CompilerParams(
-                collective_id=0, has_side_effects=True, vmem_limit_bytes=60 * 1024 * 1024
+                collective_id=0, has_side_effects=True, vmem_limit_bytes=59 * 1024 * 1024
             ),
         )(
             fields.reshape(planes),
@@ -465,7 +470,7 @@
             *small[:8],
         )
         prediction, mode_grad, field_grad = pl.pallas_call(
-            functools.partial(finish, space, dp),
+            functools.partial(finish, space),
             out_shape=(
                 jax.ShapeDtypeStruct(planes, BF),
                 jax.ShapeDtypeStruct((MODES, share * CH, CH), F32),
@@ -475,12 +480,11 @@
             out_specs=(hbm, hbm, hbm),
             scratch_shapes=[
                 pltpu.VMEM(planes, BF),
-                pltpu.VMEM((MODES, share * CH, CH), F32),
                 pltpu.VMEM((512, 128), BF),
                 pltpu.SemaphoreType.DMA((6,)),
             ],
             compiler_params=pltpu.CompilerParams(vmem_limit_bytes=32 * 1024 * 1024),
-        )(guess, part, last, team, small[6], small[8])
+        )(guess, part, last, mode, small[6], small[8])
         return (
             prediction.reshape(fields.shape),
             mode_grad.reshape(mode_weight.shape),

time: 52.5 us -> 51.3 us (0.977); the launches traced: 52.4 us -> 50.5 us
  Pallas kernels: 51.7 us -> 49.8 us
    pallas_call x1, Pallas kernels: 49 us -> 47.8 us  [local(): pl.pallas_call(functools.partial(kernel, space, dp), out_shape=(pltpu.VME...]
    pallas_call x1, Pallas kernels: 2.71 us -> 2.05 us  [local(): pl.pallas_call(functools.partial(finish, space), out_shape=(jax.ShapeDtyp...]
where the time goes in v6:
time: 51.3 us; the launch traced here: 50.5 us
  Pallas kernels  49.8 us (97%)
  between operations  0.67 us (1%)
    pallas_call x1, Pallas kernels, local(): pl.pallas_call(functools.partial(kernel, space, dp), out_shape=(pltpu.VME...  47.8 us
    pallas_call x1, Pallas kernels, local(): pl.pallas_call(functools.partial(finish, space), out_shape=(jax.ShapeDtyp...  2.05 us

profile of v6, /device:TPU:1, one launch (start us, length us, event | category | flops | bytes accessed | tf_op | source)
XLA Modules:
  0.0 50.5 jit_solution(1943294550569464388)
XLA Ops:
  0.6 0.0 copy-start
  0.6 0.0 copy-start.1
  0.7 47.8 %shard_map.175 = (bf16[32,128,128]{2,1,0:T(8,128)(2,1)S(1)}, bf16[32,128,128]{2,1,0:T(8,128)(2,1)S(1)}, f32[64,128]{1,0:T(8,128)S(1)}, f32[16,256,64]{2,1,0:T(8,128)S(1)}) custom-call(bf16[32,128,128]{2,1,0:T(8,128)(2,1)} %bitcast.7, bf16[32,128,128]{2,1,0:T(8,128)(2,1)} %bitcast.8, bf16[16,256,64]{2,1,0:T(8,128)(2,1)} %bitcast.9, ...), custom_call_target="tpu_custom_call" | custom-call | tf_op jit(solution)/shard_map/pallas_call | solution.py:404
  48.4 0.0 copy-done
  48.4 0.0 copy-done.1
  48.4 2.1 %shard_map.176 = (bf16[32,128,128]{2,1,0:T(8,128)(2,1)}, f32[16,256,64]{2,1,0:T(8,128)}, bf16[32,128,128]{2,1,0:T(8,128)(2,1)}) custom-call(bf16[32,128,128]{2,1,0:T(8,128)(2,1)S(1)} %get-tuple-element.10.pred, bf16[32,128,128]{2,1,0:T(8,128)(2,1)S(1)} %get-tuple-element.11.part, f32[64,128]{1,0:T(8,128)S(1)} %get-tuple-element.12.last_ref, ...), custom_call_target="tpu_custom_call" | custom-call | tf_op jit(solution)/shard_map/pallas_call | solution.py:472
Async XLA Ops:
  0.6 47.8 %copy-start = (bf16[256,128]{1,0:T(8,128)(2,1)S(1)}, bf16[256,128]{1,0:T(8,128)(2,1)}, u32[]{:S(2)}) copy-start(bf16[256,128]{1,0:T(8,128)(2,1)} %constant.26.clone.wavez_hbm.wavez_ref) | copy-start | bytes 196612
  0.6 47.8 %copy-start.1 = (bf16[256,32]{1,0:T(8,128)(2,1)S(1)}, bf16[256,32]{1,0:T(8,128)(2,1)}, u32[]{:S(2)}) copy-start(bf16[256,32]{1,0:T(8,128)(2,1)} %constant.28.clone.pairyt_ref) | copy-start | bytes 49156

commit v7 on v6

--- a/solution.py
+++ b/solution.py
@@ -249,7 +249,7 @@
         copy.wait()
     arrive(send2, recv2, send_sem.at[1], recv_sem.at[1], me, space)
 
-    rows_s[...] = recv2[...].astype(F32).reshape(space * 8, 128)
+    rows_s[0:space * 8, :] = recv2[...].astype(F32).reshape(space * 8, 128)
     for s in range(2):
         for b in range(share):
             block = rows_s[pl.ds(s * 4 + b, space, stride=8), :]
@@ -278,9 +278,9 @@
     def two(n, carry):
         front(2 * n + 1, pre_b)
         middle(2 * n, pre_a, grad_a)
-        back(2 * n, grad_a)
         front(jnp.minimum(2 * n + 2, tiles - 1), pre_a)
         middle(2 * n + 1, pre_b, grad_b)
+        back(2 * n, grad_a)
         back(2 * n + 1, grad_b)
         return carry
 
@@ -289,7 +289,7 @@
     for s in range(2):
         for b in range(share):
             rows_s[pl.ds(s * 4 + b, space, stride=8), :] = acc[b * space:(b + 1) * space, s * 128:(s + 1) * 128]
-    send3[...] = rows_s[...].reshape(space, 8, 128).astype(BF)
+    send3[...] = rows_s[0:space * 8, :].reshape(space, 8, 128).astype(BF)
     exchange(send3, recv3, send_sem.at[2], recv_sem.at[2], me, space)
 
     def narrow(src, dst):
@@ -416,10 +416,10 @@
                 pltpu.VMEM((MODES, share * CH, CH), BF),
                 pltpu.VMEM(planes, BF),
                 pltpu.VMEM(planes, BF),
-                pltpu.VMEM((ROWS * GRID, GRID), F32),
+                pltpu.VMEM((ROWS * GRID + GRID, GRID), F32),
                 pltpu.VMEM((ROWS, PIX), BF),
                 pltpu.VMEM((ROWS, PIX), BF),
-                pltpu.VMEM((ROWS * GRID, GRID), F32),
+                pltpu.VMEM((ROWS * GRID + GRID, GRID), F32),
                 pltpu.VMEM((512, 128), BF),
                 pltpu.VMEM((256, TILE), F32),
                 pltpu.VMEM((256, TILE), BF),
@@ -429,7 +429,7 @@
                 pltpu.VMEM((PIX // TILE, 256, TILE), BF),
                 pltpu.VMEM((256, 256), F32),
                 pltpu.VMEM((256, 256), BF),
-                pltpu.VMEM((space * 8, 128), F32),
+                pltpu.VMEM((space * 8 + 8, 128), F32),
                 pltpu.VMEM((128, 256), F32),
                 pltpu.VMEM((space, 1, 128), F32),
                 pltpu.VMEM((space, 1, 128), F32),

time: 51.3 us -> 51.2 us (level)
  no operation moved by 1% of the time
where the time goes in v7:
time: 51.2 us; the launch traced here: 50.4 us
  Pallas kernels  49.7 us (97%)
  between operations  0.67 us (1%)
    pallas_call x1, Pallas kernels, local(): pl.pallas_call(functools.partial(kernel, space, dp), out_shape=(pltpu.VME...  47.6 us
    pallas_call x1, Pallas kernels, local(): pl.pallas_call(functools.partial(finish, space), out_shape=(jax.ShapeDtyp...  2.05 us

profile of v7, /device:TPU:1, one launch (start us, length us, event | category | flops | bytes accessed | tf_op | source)
XLA Modules:
  0.0 50.4 jit_solution(15548554596757117909)
XLA Ops:
  0.6 0.0 copy-start
  0.6 0.0 copy-start.1
  0.7 47.6 %shard_map.175 = (bf16[32,128,128]{2,1,0:T(8,128)(2,1)S(1)}, bf16[32,128,128]{2,1,0:T(8,128)(2,1)S(1)}, f32[64,128]{1,0:T(8,128)S(1)}, f32[16,256,64]{2,1,0:T(8,128)S(1)}) custom-call(bf16[32,128,128]{2,1,0:T(8,128)(2,1)} %bitcast.7, bf16[32,128,128]{2,1,0:T(8,128)(2,1)} %bitcast.8, bf16[16,256,64]{2,1,0:T(8,128)(2,1)} %bitcast.9, ...), custom_call_target="tpu_custom_call" | custom-call | tf_op jit(solution)/shard_map/pallas_call | solution.py:404
  48.3 0.0 copy-done
  48.3 0.0 copy-done.1
  48.3 2.1 %shard_map.176 = (bf16[32,128,128]{2,1,0:T(8,128)(2,1)}, f32[16,256,64]{2,1,0:T(8,128)}, bf16[32,128,128]{2,1,0:T(8,128)(2,1)}) custom-call(bf16[32,128,128]{2,1,0:T(8,128)(2,1)S(1)} %get-tuple-element.10.pred, bf16[32,128,128]{2,1,0:T(8,128)(2,1)S(1)} %get-tuple-element.11.part, f32[64,128]{1,0:T(8,128)S(1)} %get-tuple-element.12.last_ref, ...), custom_call_target="tpu_custom_call" | custom-call | tf_op jit(solution)/shard_map/pallas_call | solution.py:472
Async XLA Ops:
  0.6 47.7 %copy-start = (bf16[256,128]{1,0:T(8,128)(2,1)S(1)}, bf16[256,128]{1,0:T(8,128)(2,1)}, u32[]{:S(2)}) copy-start(bf16[256,128]{1,0:T(8,128)(2,1)} %constant.26.clone.wavez_hbm.wavez_ref) | copy-start | bytes 196612
  0.6 47.7 %copy-start.1 = (bf16[256,32]{1,0:T(8,128)(2,1)S(1)}, bf16[256,32]{1,0:T(8,128)(2,1)}, u32[]{:S(2)}) copy-start(bf16[256,32]{1,0:T(8,128)(2,1)} %constant.28.clone.pairyt_ref) | copy-start | bytes 49156
